TPU v7x, 256 devices: a whole 4x4x8 slice. The times are simulated.
256 devices in a mesh: section: 8 (over x, y_hi), tensor: 32 (over z, y_lo, core).
Axes of the slice: x: 4, y: 4 (y_hi: 2, y_lo: 2; y = y_hi * 2 + y_lo), z: 8, core: 2. Of those that a mesh axis runs over, the one named last changes fastest.
Arguments:
- latent_noise: bfloat16 [128, 8, 2432], P(None, 'section'), may hold values from -6 to 6
- score_noise: bfloat16 [128, 8, 2432], P(None, 'section'), may hold values from -6 to 6
- gen_time: int32 [8], replicated, may hold values from 0 to 999
- score_time: int32 [8], replicated, may hold values from 20 to 979
- w_mod: bfloat16 [3, 256, 7296], P(None, None, 'tensor'), may hold values from -0.375 to 0.375
- w_up: bfloat16 [3, 2432, 9728], P(None, None, 'tensor'), may hold values from -0.125 to 0.125
- b_up: float32 [3, 9728], P(None, 'tensor'), may hold values from -3 to 3
- w_down: bfloat16 [3, 9728, 2432], P(None, 'tensor'), may hold values from -0.0625 to 0.0625
- b_down: float32 [3, 2432], replicated, may hold values from -3 to 3
Outputs:
- grad_w1: float32 [2432, 9728], P('section', 'tensor')
- grad_w2: float32 [9728, 2432], P('tensor', 'section')
All inputs are finite; a program needn't handle non-finite values.
Results may differ from a plain program's by a relative error of at most 0.014.
Values may be sent and summed in bfloat16 or wider, within the bound.
A program may use at most 64 MiB of HBM per device.

v0:
```python
import math

import jax
import jax.numpy as jnp
from jax import lax
from jax.sharding import PartitionSpec as P

TRAIN_STEPS = 1000


tanh_scale = math.sqrt(2.0 / math.pi)
cubic_term = 0.044715


def smooth_gate(values):
    argument = tanh_scale * (values + cubic_term * values * values * values)
    return 0.5 * values * (1.0 + jnp.tanh(argument))


def smooth_slope(values):
    argument = tanh_scale * (values + cubic_term * values * values * values)
    bent = jnp.tanh(argument)
    return 0.5 * (1.0 + bent) + 0.5 * values * (1.0 - bent * bent) * tanh_scale * (
        1.0 + 3.0 * cubic_term * values * values
    )


def embed_times(stamps, emb_width):
    half_width = emb_width // 2
    indices = jnp.arange(half_width).astype(jnp.float32)
    frequency = jnp.exp(indices * (-math.log(10000.0) / half_width))
    angles = stamps.astype(jnp.float32)[:, None] * frequency[None, :]
    return jnp.concatenate([jnp.cos(angles), jnp.sin(angles)], axis=1).astype(jnp.bfloat16)


def modulate(activations, shift_vec, scale_vec):
    values = activations.astype(jnp.float32)
    average = jnp.mean(values, axis=-1, keepdims=True)
    centred = values - average
    variance = jnp.mean(centred * centred, axis=-1, keepdims=True)
    normed = centred * lax.rsqrt(variance + 1e-06)
    return (normed * (1.0 + scale_vec) + shift_vec).astype(jnp.bfloat16)


def split_three(modulation, model_width):
    return (
        modulation[:, :model_width],
        modulation[:, model_width : 2 * model_width],
        modulation[:, 2 * model_width :],
    )


def shards(latent_noise, score_noise, gen_time, score_time, w_mod, w_up, b_up, w_down, b_down):
    token_count, samples_here, model_width = latent_noise.shape
    offset = lax.axis_index("section") * samples_here
    gen_stamp = lax.dynamic_slice_in_dim(gen_time, offset, samples_here)
    score_stamp = lax.dynamic_slice_in_dim(score_time, offset, samples_here)
    emb_gen = embed_times(gen_stamp, w_mod.shape[1])
    emb_score = embed_times(score_stamp, w_mod.shape[1])
    local_mod = jnp.stack(
        [
            jnp.dot(emb_gen, w_mod[0], preferred_element_type=jnp.float32),
            jnp.dot(emb_score, w_mod[1], preferred_element_type=jnp.float32),
            jnp.dot(emb_score, w_mod[2], preferred_element_type=jnp.float32),
        ]
    )
    modulation = lax.all_gather(local_mod, "tensor", axis=2, tiled=True)
    gen_shift, gen_scale, gen_gate = split_three(modulation[0], model_width)
    real_shift, real_scale, real_gate = split_three(modulation[1], model_width)
    fake_shift, fake_scale, fake_gate = split_three(modulation[2], model_width)
    noise_level = (score_stamp.astype(jnp.float32) / TRAIN_STEPS)[None, :, None]
    share_rows = token_count // lax.axis_size("tensor")
    first_share = lax.axis_index("tensor") * share_rows

    def hidden_of(inputs, network):
        preact = (
            jnp.einsum("tbd,df->tbf", inputs, w_up[network], preferred_element_type=jnp.float32)
            + b_up[network]
        )
        return (preact, smooth_gate(preact).astype(jnp.bfloat16))

    def down_of(hidden, network):
        return jnp.einsum(
            "tbf,fd->tbd", hidden, w_down[network], preferred_element_type=jnp.float32
        )

    gen_inputs = modulate(latent_noise, gen_shift, gen_scale)
    gen_preact, hidden_gen = hidden_of(gen_inputs, 0)
    gen_share = lax.psum_scatter(
        down_of(hidden_gen, 0).astype(jnp.bfloat16), "tensor", scatter_dimension=0, tiled=True
    ).astype(jnp.float32)
    latent_share = lax.dynamic_slice_in_dim(latent_noise, first_share, share_rows, 0)
    noise_share = lax.dynamic_slice_in_dim(score_noise, first_share, share_rows, 0)
    generated = latent_share.astype(jnp.float32) + gen_gate * (gen_share + b_down[0])
    noised_share = (
        (1.0 - noise_level) * generated + noise_level * noise_share.astype(jnp.float32)
    ).astype(jnp.bfloat16)
    noised = lax.all_gather(noised_share, "tensor", axis=0, tiled=True)
    real_pre, hidden_real = hidden_of(modulate(noised, real_shift, real_scale), 1)
    fake_pre, hidden_fake = hidden_of(modulate(noised, fake_shift, fake_scale), 2)
    total_rows = samples_here * lax.axis_size("section") * token_count
    root_rows = math.sqrt(total_rows)
    bias_gap = fake_gate * b_down[2] - real_gate * b_down[1]
    gap_term = fake_gate * down_of(hidden_fake, 2) - real_gate * down_of(hidden_real, 1)
    gap_sum = lax.psum(gap_term.astype(jnp.bfloat16), "tensor").astype(jnp.float32)
    contrast = gap_sum + bias_gap
    output_grad = (contrast / root_rows * gen_gate).astype(jnp.bfloat16)
    hidden_grad = jnp.einsum(
        "tbd,fd->tbf", output_grad, w_down[0], preferred_element_type=jnp.float32
    )
    preact_grad = (hidden_grad * smooth_slope(gen_preact)).astype(jnp.bfloat16)
    down_local = jnp.einsum(
        "tbf,tbd->fd", hidden_gen, output_grad, preferred_element_type=jnp.float32
    )
    grad_w2 = lax.psum_scatter(
        down_local.astype(jnp.bfloat16), "section", scatter_dimension=1, tiled=True
    ).astype(jnp.float32)
    grad_w1 = lax.psum_scatter(
        jnp.einsum(
            "tbd,tbf->df", gen_inputs, preact_grad, preferred_element_type=jnp.float32
        ).astype(jnp.bfloat16),
        "section",
        scatter_dimension=0,
        tiled=True,
    ).astype(jnp.float32)
    return (grad_w1, grad_w2)


def solution(mesh):
    placed = (
        P(None, "section", None),
        P(None, "section", None),
        P(),
        P(),
        P(None, None, "tensor"),
        P(None, None, "tensor"),
        P(None, "tensor"),
        P(None, "tensor", None),
        P(),
    )
    return jax.shard_map(
        shards,
        mesh=mesh,
        in_specs=placed,
        out_specs=(P("section", "tensor"), P("tensor", "section")),
        check_vma=False,
    )
```

profile of v0, /device:TPU:1, one launch (start us, length us, event | category | flops | bytes accessed | tf_op | source)
XLA Modules:
  0.0 949.3 jit_solution(5904612919459939075)
XLA Ops:
  7.2 0.0 all-reduce.6.cloned.1.call-start
  7.2 1.2 dynamic_slice.13
  9.2 1.0 convolution_bitcast_fusion
  10.2 1.1 convolution_bitcast_fusion.1
  11.3 1.3 dynamic_slice.12
  13.3 1.0 convolution_bitcast_fusion.2
  14.4 0.2 copy.12
  14.5 59.1 %all_gather.6 = f32[3,1,7296]{0,1,2:T(1,128)S(1)} all-gather(f32[3,1,228]{0,1,2:T(1,128)S(1)} %copy.12), channel_id=1, replica_groups=mesh['section'=8,'tensor'=32] {'tensor'}, dimensions={2}, use_global_device_ids=true | all-gather | bytes 90288 | tf_op jit(solution)/shard_map/all_gather | solution.py:67
  73.7 0.0 copy-start.3
  73.7 0.0 copy-start
  73.7 213.9 %slice_reduce_fusion.1 = (f32[7296]{0:T(1024)S(1)}, f32[7296]{0:T(1024)S(1)}, f32[7296]{0:T(1024)S(1)}) fusion(f32[3,1,7296]{0,1,2:T(1,128)S(1)} %all_gather.6), kind=kLoop, calls=%fused_computation.6 | loop fusion | bytes 175104 | tf_op jit(solution)/shard_map/slice | solution.py:70
  287.6 0.0 copy-done.3
  287.6 0.1 slice_reduce_fusion.5
  287.7 0.0 copy-done
  287.7 0.2 convert_reduce_fusion.1
  287.9 0.3 fusion.33
  288.2 2.0 fusion.37
  290.3 0.0 copy-start.4
  290.3 0.0 copy-start.2
  290.3 2.8 fusion.2
  293.1 0.0 all-reduce.6.cloned.1.call-update
  293.1 0.0 all-reduce.4.cloned.1.call-start
  293.2 0.0 copy-done.4
  293.3 0.6 dynamic-slice
  294.5 0.0 copy-done.2
  294.5 0.2 subtract_reduce_fusion
  294.7 218.5 %all-reduce.6.cloned.1.call-done = bf16[128,1,2432]{2,0,1:T(8,128)(2,1)} async-done(((bf16[128,1,2432]{2,0,1:T(8,128)(2,1)}), bf16[128,1,2432]{2,0,1:T(8,128)(2,1)}) %all-reduce.6.cloned.1.call-update) | async-done | bytes 622608
  513.2 0.8 add_convert_fusion
  514.1 37.4 %all_gather.7 = bf16[128,1,2432]{2,1,0:T(2,128)(2,1)S(1)} all-gather(bf16[4,1,2432]{2,1,0:T(2,128)(2,1)S(1)} %copy.13), channel_id=1, replica_groups=mesh['section'=8,'tensor'=32] {'tensor'}, dimensions={0}, use_global_device_ids=true | all-gather | bytes 642048 | tf_op jit(solution)/shard_map/all_gather | solution.py:98
  551.5 0.2 convert_reduce_fusion
  551.7 0.3 fusion.32
  552.1 3.0 convolution_multiply_fusion
  555.1 3.8 fusion.3
  558.9 0.0 all-reduce.4.cloned.1.call-update
  558.9 0.0 reduce-scatter.8.cloned.1.call-start
  559.0 216.6 %all-reduce.4.cloned.1.call-done = bf16[128,1,2432]{2,0,1:T(8,128)(2,1)} async-done(((bf16[128,1,2432]{2,0,1:T(8,128)(2,1)}), bf16[128,1,2432]{2,0,1:T(8,128)(2,1)}) %all-reduce.4.cloned.1.call-update) | async-done | bytes 622608 | tf_op jit(solution)/shard_map/psum | solution.py:105
  775.6 1.7 convolution_convert_fusion.1
  777.3 2.5 copy.17
  779.8 0.0 copy-start.1
  779.8 0.0 reduce-scatter.8.cloned.1.call-update
  779.8 0.0 reduce-scatter.6.cloned.1.call-start
  779.8 1.0 copy-done.1
  780.8 4.6 convolution_convert_fusion
  785.4 0.0 reduce-scatter.6.cloned.1.call-update
  785.5 74.2 %reduce-scatter.8.cloned.1.call-done = bf16[304,304]{1,0:T(8,128)(2,1)} async-done(((bf16[2432,304]{1,0:T(8,128)(2,1)}), bf16[304,304]{1,0:T(8,128)(2,1)}) %reduce-scatter.8.cloned.1.call-update) | async-done | bytes 184848
  859.7 1.1 copy.18
  860.8 0.8 convert_element_type.129
  861.6 79.5 %reduce-scatter.6.cloned.1.call-done = bf16[304,304]{1,0:T(8,128)(2,1)} async-done(((bf16[2432,304]{1,0:T(8,128)(2,1)}), bf16[304,304]{1,0:T(8,128)(2,1)}) %reduce-scatter.6.cloned.1.call-update) | async-done | bytes 184848 | tf_op jit(solution)/shard_map/reduce_scatter | solution.py:118
  941.1 1.7 convert_element_type.127
  (17 shorter events, 0.3 us)
Async XLA Ops:
  7.2 506.1 %all-reduce.6.cloned.1.call-start = ((), (), s32[]{:S(2)}) async-start(), calls=%async_computation.5 | async-start | bytes 1245184
  73.7 213.9 %copy-start.3 = (f32[3,304]{1,0:T(4,128)S(1)}, f32[3,304]{1,0:T(4,128)}, u32[]{:S(2)}) copy-start(f32[3,304]{1,0:T(4,128)} %param.15) | copy-start | bytes 10948
  73.7 214.0 %copy-start = (bf16[128,1,2432]{2,0,1:T(8,128)(2,1)S(1)}, bf16[128,1,2432]{2,0,1:T(8,128)(2,1)}, u32[]{:S(2)}) copy-start(bf16[128,1,2432]{2,0,1:T(8,128)(2,1)} %param.9) | copy-start | bytes 1867780
  290.3 3.0 copy-start.4
  290.3 4.2 copy-start.2
  293.1 482.5 %all-reduce.4.cloned.1.call-start = ((), (), s32[]{:S(2)}) async-start(), calls=%async_computation.2 | async-start | bytes 1245184 | tf_op jit(solution)/shard_map/psum | solution.py:105
  558.9 300.7 %reduce-scatter.8.cloned.1.call-start = ((), (), s32[]{:S(2)}) async-start(), calls=%async_computation.4 | async-start | bytes 2101248
  779.8 1.1 copy-start.1
  779.8 161.3 %reduce-scatter.6.cloned.1.call-start = ((), (), s32[]{:S(2)}) async-start(), calls=%async_computation.3 | async-start | bytes 2101248 | tf_op jit(solution)/shard_map/reduce_scatter | solution.py:118
Sparse Core Ops, SparseCore 0:
  293.2 219.9 all-reduce.5
  559.1 216.5 all-reduce.3
  779.9 79.6 reduce-scatter.7
  863.6 77.4 reduce-scatter.5
where the time goes:
time: 950 us; the launch traced here: 949 us
  waiting for transfers between devices  589 us (62%)
  local copies, waits for them, and re-layouts  222 us (23%)
  blocking collectives  96.6 us (10%)
  matrix products  21.1 us (2%)
  between operations  15.9 us (2%)
    unnamed x6, waiting for transfers between devices  293 us
    psum x1, waiting for transfers between devices, shards(): lax.psum(gap_term.astype(jnp.bfloat16), 'tensor').astype(jnp.float32)  217 us
    slice x1, local copies, waits for them, and re-layouts, shards(): fake_shift, fake_scale, fake_gate = split_three(modulation[2], model_width)  214 us
    reduce_scatter x1, waiting for transfers between devices, shards(): lax.psum_scatter(jnp.einsum('tbd,tbf->df', gen_inputs, preact_grad, prefe...  79.5 us
    all_gather x1, blocking collectives, shards(): modulation = lax.all_gather(local_mod, 'tensor', axis=2, tiled=True)  59.1 us
    all_gather x1, blocking collectives, shards(): noised = lax.all_gather(noised_share, 'tensor', axis=0, tiled=True)  37.4 us
  transfers between devices with their start and end apart: 4, of which 4 were waited for; matrix products, arithmetic and copies ran while one was open for 1% of the time, Pallas kernels for 0%

commit v1 on v0

v1 whole, which is shorter than its diff:
```python
import functools
import math

import jax
import jax.numpy as jnp
from jax import lax
from jax.experimental import pallas as pl
from jax.experimental.pallas import tpu as pltpu
from jax.sharding import PartitionSpec as P

TRAIN_STEPS = 1000
MESH = pl.DeviceIdType.MESH
f32 = jnp.float32
bf16 = jnp.bfloat16

NT = (((1,), (1,)), ((), ()))
NN = (((1,), (0,)), ((), ()))

tanh_scale = math.sqrt(2.0 / math.pi)
cubic_term = 0.044715

TOK = 128
D = 2432
DP = 2560
F = 304
MODC = 228
WIDTHS = (384, 256)
BASES = tuple(4 * sum(WIDTHS[:j]) for j in range(len(WIDTHS)))
NCH = len(WIDTHS)

CHIPS = [
    (dz, dy) for dz in (4, 3, 5, 2, 6, 1, 7, 0) for dy in (1, 0) if (dz, dy) != (0, 0)
]
SECTS = [(2, 1), (1, 1), (3, 1), (2, 0), (0, 1), (1, 0), (3, 0)]


def mul(value, factor):
    return pl.multiple_of(value * factor, factor)


def dot(a, b, dims):
    return lax.dot_general(a, b, dims, preferred_element_type=f32)


def gelu(v):
    return 0.5 * v * (1.0 + jnp.tanh(tanh_scale * (v + cubic_term * v * v * v)))


def slope(v):
    bent = jnp.tanh(tanh_scale * (v + cubic_term * v * v * v))
    return 0.5 * (1.0 + bent) + 0.5 * v * (1.0 - bent * bent) * tanh_scale * (
        1.0 + 3.0 * cubic_term * v * v
    )


class Sems:
    def __init__(self):
        self.count = 0

    def take(self, n):
        first = self.count
        self.count += n
        return first


SEMS = Sems()
LOAD = SEMS.take(16)
MX_S, MX_R = SEMS.take(1), SEMS.take(1)
MA_S, MA_R = SEMS.take(15), SEMS.take(15)
CX_S, CX_R = SEMS.take(4 * NCH), SEMS.take(4 * NCH)
RS_S, RS_R = SEMS.take(30 * NCH), SEMS.take(30 * NCH)
AG_S, AG_R = SEMS.take(30 * NCH), SEMS.take(30 * NCH)
FW_S, FW_R = SEMS.take(32 * NCH), SEMS.take(32 * NCH)
SX_S, SX_R = SEMS.take(28), SEMS.take(28)


def kernel(
    lat, noi, gt, st, wmod, wup, bup, wdn, bdn, o1, o2,
    latv, noiv, wmodv, wupv, wdnv, bupv, bdnv,
    mblk, mpart, mcomb, mall, modv,
    xn, xm, hid, prev, slope_t,
    psend, precv, csum, rsrecv, nbuf, gbuf,
    gen_t, og_t, g_all, h_all, p_all, o_all, pg, hid_t, res,
    sem,
):
    s = lax.axis_index("section")
    t = lax.axis_index("tensor")
    x, yh = s // 2, s % 2
    z, yl, c = t // 4, (t // 2) % 2, t % 2
    q = yl * 2 + c

    def chip_at(dz, dy):
        return lax.rem(z + dz, 8), lax.rem(yl + dy, 2)

    def chip_dev(dz, dy):
        z2, y2 = chip_at(dz, dy)
        return (s, z2 * 4 + y2 * 2 + c)

    def sect_at(dx, dy):
        return lax.rem(x + dx, 4) * 2 + lax.rem(yh + dy, 2)

    partner = (s, z * 4 + yl * 2 + (1 - c))

    def remote(src, dst, ssem, rsem, dev):
        return pltpu.make_async_remote_copy(
            src_ref=src, dst_ref=dst, send_sem=sem.at[ssem], recv_sem=sem.at[rsem],
            device_id=dev, device_id_type=MESH,
        )

    def load(k, src, dst):
        copy = pltpu.make_async_copy(src, dst, sem.at[LOAD + k])
        copy.start()
        return copy

    ld_wmod = load(0, wmod, wmodv)
    ld_lat = load(1, lat, latv.at[:, 0:D])
    ld_up = [load(2, wup.at[0], wupv.at[0])]
    ld_bup = load(3, bup, bupv)
    ld_dn = [load(4, wdn.at[0], wdnv.at[0])]
    ld_bdn = load(5, bdn, bdnv.at[:, 0:D])
    ld_noi = load(6, noi, noiv.at[:, 0:D])
    for n in (1, 2):
        ld_up.append(load(5 + 2 * n, wup.at[n], wupv.at[n]))
        ld_dn.append(load(6 + 2 * n, wdn.at[n], wdnv.at[n]))

    barrier = pltpu.get_barrier_semaphore()
    for dz, dy in CHIPS:
        pl.semaphore_signal(barrier, inc=1, device_id=chip_dev(dz, dy), device_id_type=MESH)
    for dx, dy in SECTS:
        pl.semaphore_signal(barrier, inc=1, device_id=(sect_at(dx, dy), t), device_id_type=MESH)
    pl.semaphore_signal(barrier, inc=1, device_id=partner, device_id_type=MESH)

    lane = lax.broadcasted_iota(jnp.int32, (8, 128), 1).astype(f32)
    freq = jnp.exp(lane * (-math.log(10000.0) / 128))

    def embed(stamp):
        angle = stamp.astype(f32) * freq
        return jnp.concatenate([jnp.cos(angle), jnp.sin(angle)], axis=1).astype(bf16)

    emb_gen = embed(gt[s])
    emb_score = embed(st[s])
    sigma = st[s].astype(f32) / TRAIN_STEPS
    ld_wmod.wait()
    row = lax.broadcasted_iota(jnp.int32, (8, MODC), 0)
    m0 = dot(emb_gen, wmodv[0], NT)
    m1 = dot(emb_score, wmodv[1], NT)
    m2 = dot(emb_score, wmodv[2], NT)
    mblk[...] = jnp.zeros_like(mblk)
    mblk[:, 0:MODC] = jnp.where(
        row % 4 == 0, m0, jnp.where(row % 4 == 1, m1, jnp.where(row % 4 == 2, m2, 0.0))
    )
    modv[...] = jnp.zeros_like(modv)
    pl.semaphore_wait(barrier, 23)

    mx = remote(mblk, mpart, MX_S, MX_R, partner)
    mx.start()
    mx.wait_recv()
    row8 = lax.broadcasted_iota(jnp.int32, (8, 256), 0)
    mcomb[...] = jnp.where((row8 < 4) == (c == 0), mblk[...], mpart[...])
    chip = z * 2 + yl
    ma = []
    for k, (dz, dy) in enumerate(CHIPS):
        copy = remote(mcomb, mall.at[chip], MA_S + k, MA_R + k, chip_dev(dz, dy))
        copy.start()
        ma.append(copy)
    mall[chip] = mcomb[...]

    latv[:, D:DP] = jnp.zeros((TOK, DP - D), bf16)
    noiv[:, D:DP] = jnp.zeros((TOK, DP - D), bf16)
    bdnv[:, D:DP] = jnp.zeros((3, DP - D), f32)
    ld_lat.wait()

    def norm_rows(values):
        mean = jnp.mean(values, axis=1, keepdims=True)
        centred = values - mean
        var = jnp.mean(centred * centred, axis=1, keepdims=True)
        return centred * lax.rsqrt(var + 1e-06)

    def norm_body(i, _):
        rows = pl.ds(mul(i, 16), 16)
        xn[rows, :] = norm_rows(latv[rows, 0:D].astype(f32))
        return 0

    lax.fori_loop(0, 8, norm_body, 0)
    for copy in ma:
        copy.wait_recv()
    for k in range(32):
        modv[0:3, MODC * k : MODC * (k + 1)] = mall[k // 2, 4 * (k % 2) : 4 * (k % 2) + 3, 0:MODC]

    def gen_body(i, _):
        rows = pl.ds(mul(i, 16), 16)
        xm[0, rows, :] = (xn[rows, :] * (1.0 + modv[0:1, D : 2 * D]) + modv[0:1, 0:D]).astype(bf16)
        return 0

    lax.fori_loop(0, 8, gen_body, 0)
    ld_up[0].wait()
    ld_bup.wait()
    pre = dot(xm[0], wupv[0], NT) + bupv[0:1, :]
    prev[:, 0:F] = pre
    hid[0] = gelu(pre).astype(bf16)
    ld_dn[0].wait()

    def chunk_cols(j):
        return BASES[j], min(BASES[j] + 4 * WIDTHS[j], D)

    def all_reduce(a, produce, finish, out, between):
        def core_copy(j, i):
            col = mul(BASES[j] // 128 + (i * 2 + 1 - c) * (WIDTHS[j] // 128), 128)
            k = (a * NCH + j) * 2 + i
            return remote(
                psend.at[a, :, pl.ds(col, WIDTHS[j])], precv[a][j].at[i], CX_S + k, CX_R + k, partner
            )

        def scatter(j, k):
            z2, y2 = chip_at(*CHIPS[k])
            i = (a * NCH + j) * 15 + k
            return remote(
                csum[a][j].at[y2, pl.ds(mul(z2, 16), 16), :], rsrecv[a][j].at[k],
                RS_S + i, RS_R + i, chip_dev(*CHIPS[k]),
            )

        def piece(ref, j, z2, y2):
            col = mul(BASES[j] // 128 + (y2 * 2 + c) * (WIDTHS[j] // 128), 128)
            return ref.at[pl.ds(mul(z2, 16), 16), pl.ds(col, WIDTHS[j])]

        def gather(j, k):
            own = piece(out, j, z, yl)
            i = (a * NCH + j) * 15 + k
            return remote(own, own, AG_S + i, AG_R + i, chip_dev(*CHIPS[k]))

        def forward(j, k):
            dz, dy = CHIPS[k] if k < 15 else (0, 0)
            z2, y2 = chip_at((8 - dz) % 8, dy)
            part = piece(out, j, z2, y2)
            i = (a * NCH + j) * 16 + k
            return remote(part, part, FW_S + i, FW_R + i, partner)

        def send_chunk(j):
            for i in range(2):
                core_copy(j, i).wait_recv()
            for i in range(2):
                col = mul(BASES[j] // 128 + (i * 2 + c) * (WIDTHS[j] // 128), 128)
                csum[a][j][i] = (
                    psend[a, :, pl.ds(col, WIDTHS[j])].astype(f32) + precv[a][j][i].astype(f32)
                ).astype(bf16)
            for k in range(15):
                scatter(j, k).start()

        for j in range(NCH):
            produce(j)
            for i in range(2):
                core_copy(j, i).start()
            if j >= 1:
                send_chunk(j - 1)
        send_chunk(NCH - 1)
        between()
        for j in range(NCH):
            total = csum[a][j][yl, pl.ds(mul(z, 16), 16), :].astype(f32)
            for k in reversed(range(15)):
                scatter(j, k).wait_recv()
                total = total + rsrecv[a][j][k].astype(f32)
            col = mul(BASES[j] // 128 + q * (WIDTHS[j] // 128), 128)
            piece(out, j, z, yl)[...] = finish(total, pl.ds(mul(z, 16), 16), col, WIDTHS[j])
            for k in range(15):
                gather(j, k).start()
            forward(j, 15).start()
        for j in range(NCH):
            for k in reversed(range(15)):
                gather(j, k).wait_recv()
                forward(j, k).start()
        for j in range(NCH):
            for k in reversed(range(16)):
                forward(j, k).wait_recv()

        def drain():
            for j in range(NCH):
                for i in range(2):
                    core_copy(j, i).wait_send()
                for k in range(15):
                    scatter(j, k).wait_send()
                    gather(j, k).wait_send()
                for k in range(16):
                    forward(j, k).wait_send()

        return drain

    def produce_gen(j):
        lo, hi = chunk_cols(j)
        psend[0, :, lo:hi] = dot(hid[0], wdnv[0, :, lo:hi], NN).astype(bf16)
        if hi < BASES[j] + 4 * WIDTHS[j]:
            psend[0, :, hi:DP] = jnp.zeros((TOK, DP - hi), bf16)

    def finish_gen(total, rows, col, width):
        cols = pl.ds(col, width)
        gate = modv[0:1, pl.ds(pl.multiple_of(2 * D + col, 128), width)]
        generated = latv[rows, cols].astype(f32) + gate * (total + bdnv[0:1, cols])
        return (
            (1.0 - sigma) * generated + sigma * noiv[rows, cols].astype(f32)
        ).astype(bf16)

    def sect_copy(part, k):
        dev = (sect_at(*SECTS[k]), t)
        i = part * 7 + k
        rows = pl.ds(mul(dev[0], F // 16 * 16), F)
        src = (gen_t.at[rows, :], hid_t, pg, og_t.at[rows, :])[part]
        dst = (g_all, h_all, p_all, o_all)[part].at[:, pl.ds(mul(s, 128), 128)]
        return remote(src, dst, SX_S + i, SX_R + i, dev)

    def transposed(value):
        return value.astype(f32).T

    def early_sends():
        ld_bdn.wait()
        ld_noi.wait()
        for b in range(19):
            cols = slice(128 * b, 128 * b + 128)
            gen_t[cols, :] = transposed(xm[0, :, cols]).astype(bf16)
        for k in range(7):
            sect_copy(0, k).start()
        g_all[:, pl.ds(mul(s, 128), 128)] = gen_t[pl.ds(mul(s, F), F), :]
        prev[:, F:384] = jnp.zeros((TOK, 384 - F), f32)
        for b in range(3):
            height = min(128, F - 128 * b)
            block = prev[:, 128 * b : 128 * b + 128].T
            slope_t[128 * b : 128 * b + height, :] = slope(block)[0:height]
            hid_t[128 * b : 128 * b + height, :] = gelu(block)[0:height].astype(bf16)
        for k in range(7):
            sect_copy(1, k).start()
        h_all[:, pl.ds(mul(s, 128), 128)] = hid_t[...]

    drain_gen = all_reduce(0, produce_gen, finish_gen, nbuf, early_sends)

    def score_body(i, _):
        rows = pl.ds(mul(i, 16), 16)
        normed = norm_rows(nbuf[rows, 0:D].astype(f32))
        for n in (1, 2):
            xm[n, rows, :] = (normed * (1.0 + modv[n : n + 1, D : 2 * D]) + modv[n : n + 1, 0:D]).astype(bf16)
        return 0

    lax.fori_loop(0, 8, score_body, 0)
    for n in (1, 2):
        ld_up[n].wait()
        hid[n] = gelu(dot(xm[n], wupv[n], NT) + bupv[n : n + 1, :]).astype(bf16)
    for n in (1, 2):
        ld_dn[n].wait()

    def produce_gap(j):
        lo, hi = chunk_cols(j)
        real = dot(hid[1], wdnv[1, :, lo:hi], NN) * modv[1:2, 2 * D + lo : 2 * D + hi]
        fake = dot(hid[2], wdnv[2, :, lo:hi], NN) * modv[2:3, 2 * D + lo : 2 * D + hi]
        psend[1, :, lo:hi] = (fake - real).astype(bf16)
        if hi < BASES[j] + 4 * WIDTHS[j]:
            psend[1, :, hi:DP] = jnp.zeros((TOK, DP - hi), bf16)

    def finish_gap(total, rows, col, width):
        cols = pl.ds(col, width)
        gates = modv[0:3, pl.ds(pl.multiple_of(2 * D + col, 128), width)]
        bias = gates[2:3] * bdnv[2:3, cols] - gates[1:2] * bdnv[1:2, cols]
        return ((total + bias) / 32.0 * gates[0:1]).astype(bf16)

    def drain_first():
        mx.wait_send()
        for copy in ma:
            copy.wait_send()
        drain_gen()
        for part in (0, 1):
            for k in range(7):
                sect_copy(part, k).wait_send()

    drain_gap = all_reduce(1, produce_gap, finish_gap, gbuf, drain_first)

    pg[...] = (dot(wdnv[0], gbuf[:, 0:D], NT) * slope_t[...]).astype(bf16)
    for k in range(7):
        sect_copy(2, k).start()
    p_all[:, pl.ds(mul(s, 128), 128)] = pg[...]
    for b in range(19):
        cols = slice(128 * b, 128 * b + 128)
        og_t[cols, :] = transposed(gbuf[:, cols]).astype(bf16)
    for k in range(7):
        sect_copy(3, k).start()
    o_all[:, pl.ds(mul(s, 128), 128)] = og_t[pl.ds(mul(s, F), F), :]
    drain_gap()
    for part in (0, 2):
        for k in reversed(range(7)):
            sect_copy(part, k).wait_recv()
    res[0] = dot(g_all[...], p_all[...], NT)
    out1 = pltpu.make_async_copy(res.at[0], o1, sem.at[LOAD + 12])
    out1.start()
    for part in (1, 3):
        for k in reversed(range(7)):
            sect_copy(part, k).wait_recv()
    res[1] = dot(h_all[...], o_all[...], NT)
    out2 = pltpu.make_async_copy(res.at[1], o2, sem.at[LOAD + 13])
    out2.start()
    for part in (2, 3):
        for k in range(7):
            sect_copy(part, k).wait_send()
    out1.wait()
    out2.wait()


def shards(latent_noise, score_noise, gen_time, score_time, w_mod, w_up, b_up, w_down, b_down):
    anywhere = pl.BlockSpec(memory_space=pl.ANY)
    scalars = pl.BlockSpec(memory_space=pltpu.SMEM)
    vm = pltpu.VMEM
    per_chunk = lambda lead: [[vm((lead, TOK, w), bf16) for w in WIDTHS] for _ in range(2)]
    scratch = [
        vm((TOK, DP), bf16), vm((TOK, DP), bf16), vm((3, MODC, 256), bf16),
        vm((3, F, D), bf16), vm((3, F, D), bf16), vm((3, F), f32), vm((3, DP), f32),
        vm((8, 256), f32), vm((8, 256), f32), vm((8, 256), f32), vm((16, 8, 256), f32),
        vm((8, 7424), f32),
        vm((TOK, D), f32), vm((3, TOK, D), bf16), vm((3, TOK, F), bf16), vm((TOK, 384), f32),
        vm((F, TOK), f32),
        vm((2, TOK, DP), bf16), per_chunk(2), per_chunk(2),
        [[vm((15, 16, w), bf16) for w in WIDTHS] for _ in range(2)],
        vm((TOK, DP), bf16), vm((TOK, DP), bf16),
        vm((D, TOK), bf16), vm((D, TOK), bf16),
        vm((F, 1024), bf16), vm((F, 1024), bf16), vm((F, 1024), bf16), vm((F, 1024), bf16),
        vm((F, TOK), bf16), vm((F, TOK), bf16), vm((2, F, F), f32),
        pltpu.SemaphoreType.DMA((SEMS.count,)),
    ]
    out = jax.ShapeDtypeStruct((F, F), f32)
    return pl.pallas_call(
        kernel,
        out_shape=(out, out),
        in_specs=[anywhere, anywhere, scalars, scalars] + [anywhere] * 5,
        out_specs=(anywhere, anywhere),
        scratch_shapes=scratch,
        cost_estimate=pl.CostEstimate(flops=1_700_000_000, bytes_accessed=11_000_000, transcendentals=300_000),
        compiler_params=pltpu.CompilerParams(
            collective_id=0, has_side_effects=True, vmem_limit_bytes=56 * 2**20
        ),
    )(
        latent_noise.reshape(TOK, D), score_noise.reshape(TOK, D), gen_time, score_time,
        w_mod.transpose(0, 2, 1), w_up.transpose(0, 2, 1), b_up, w_down, b_down,
    )


def solution(mesh):
    placed = (
        P(None, "section", None),
        P(None, "section", None),
        P(),
        P(),
        P(None, None, "tensor"),
        P(None, None, "tensor"),
        P(None, "tensor"),
        P(None, "tensor", None),
        P(),
    )
    return jax.shard_map(
        shards,
        mesh=mesh,
        in_specs=placed,
        out_specs=(P("section", "tensor"), P("tensor", "section")),
        check_vma=False,
    )
```

time: 950 us -> 96.9 us (0.10)
  waiting for transfers between devices: 589 us -> 0 us
  local copies, waits for them, and re-layouts: 222 us -> 3.64 us
  blocking collectives: 96.6 us -> 0 us
  Pallas kernels: 0 us -> 92.4 us
  matrix products: 21.1 us -> 0 us
  between operations: 15.9 us -> 0.64 us
    unnamed x6 -> x0, waiting for transfers between devices: 293 us -> none
    psum x1 -> x0, waiting for transfers between devices: 217 us -> none  [shards(): lax.psum(gap_term.astype(jnp.bfloat16), 'tensor').astype(jnp.float32)]
    slice x2 -> x0, local copies, waits for them, and re-layouts: 214 us -> none  [the longest x1 214 us: shards(): fake_shift, fake_scale, fake_gate = split_three(modulation[2], model_width)]
    all_gather x2 -> x0, blocking collectives: 96.6 us -> none  [the longest x1 59.1 us: shards(): modulation = lax.all_gather(local_mod, 'tensor', axis=2, tiled=True)]
    pallas_call x0 -> x1, Pallas kernels: none -> 92.4 us  [shards(): pl.pallas_call(kernel, out_shape=(out, out), in_specs=[anywhere, anywhere...]
    reduce_scatter x1 -> x0, waiting for transfers between devices: 79.5 us -> none  [shards(): lax.psum_scatter(jnp.einsum('tbd,tbf->df', gen_inputs, preact_grad, prefe...]
    dot_general x9 -> x0, matrix products: 21.1 us -> none  [the longest x3 9.63 us: down_of(): jnp.einsum('tbf,fd->tbd', hidden, w_down[network], preferred_element_type...]
  transfers between devices with their start and end apart: 4 -> 0, of which waited for: 4 -> 0; matrix products, arithmetic and copies ran while one was open for 1% -> 0% of each run, Pallas kernels for 0% -> 0%
where the time goes in v1:
time: 96.9 us; the launch traced here: 96.7 us
  Pallas kernels  92.4 us (95%)
  local copies, waits for them, and re-layouts  3.64 us (4%)
    pallas_call x1, Pallas kernels, shards(): pl.pallas_call(kernel, out_shape=(out, out), in_specs=[anywhere, anywhere...  92.4 us
    unnamed x2, local copies, waits for them, and re-layouts  3.64 us

profile of v1, /device:TPU:1, one launch (start us, length us, event | category | flops | bytes accessed | tf_op | source)
XLA Modules:
  0.0 96.7 jit_solution(11894284368062469581)
XLA Ops:
  0.6 92.4 %shard_map.104 = (f32[304,304]{1,0:T(8,128)}, f32[304,304]{1,0:T(8,128)}) custom-call(bf16[128,2432]{1,0:T(8,128)(2,1)} %bitcast.5, bf16[128,2432]{1,0:T(8,128)(2,1)} %bitcast.6, s32[8]{0:T(128)} %gt.1, s32[8]{0:T(128)} %st.1, bf16[3,228,256]{2,1,0:T(8,128)(2,1)} %bitcast.7, bf16[3,304,2432]{2,1,0:T(8,128)(2,1)} %bitcast.4, f32[3,304]{1,0:T(4,128)} %bup.1, ...), custom_call_target="tpu_custom_call" | custom-call | flops 1700000000 | bytes 11000000 | tf_op jit(solution)/shard_map/pallas_call | solution.py:423
  93.0 1.8 %copy.13 = f32[304,304]{1,0:T(8,128)} copy(f32[304,304]{1,0:T(8,128)} %get-tuple-element.4) | data formatting | bytes 739328
  94.9 1.8 %copy.14 = f32[304,304]{1,0:T(8,128)} copy(f32[304,304]{1,0:T(8,128)} %get-tuple-element.5) | data formatting | bytes 739328

commit v2 on v1

v2 whole, which is shorter than its diff:
```python
import functools
import math

import jax
import jax.numpy as jnp
from jax import lax
from jax.experimental import pallas as pl
from jax.experimental.pallas import tpu as pltpu
from jax.sharding import PartitionSpec as P

TRAIN_STEPS = 1000
MESH = pl.DeviceIdType.MESH
f32 = jnp.float32
bf16 = jnp.bfloat16

NT = (((1,), (1,)), ((), ()))
NN = (((1,), (0,)), ((), ()))

tanh_scale = math.sqrt(2.0 / math.pi)
cubic_term = 0.044715

TOK = 128
D = 2432
DP = 2560
F = 304
MODC = 228
WIDTHS = (384, 256)
BASES = tuple(4 * sum(WIDTHS[:j]) for j in range(len(WIDTHS)))
NCH = len(WIDTHS)
STOP = 99
COPY_OUT = 0
BG = 1
LATE = 0
GRAD = bf16 if COPY_OUT else f32

DISTANCES = (0, 1, 7, 2, 6, 3, 5, 4)
CORES = [(dz, dy, dc) for dz in reversed(DISTANCES) for dy in (1, 0) for dc in (0, 1) if (dz, dy, dc) != (0, 0, 0)]
CHIPS = [(dz, dy) for dz in reversed(DISTANCES) for dy in (1, 0) if (dz, dy) != (0, 0)]
SECTS = [(2, 1), (1, 1), (3, 1), (2, 0), (0, 1), (1, 0), (3, 0)]


def mul(value, factor):
    return pl.multiple_of(value * factor, factor)


def dot(a, b, dims):
    return lax.dot_general(a, b, dims, preferred_element_type=f32)


def gelu(v):
    return 0.5 * v * (1.0 + jnp.tanh(tanh_scale * (v + cubic_term * v * v * v)))


def slope(v):
    bent = jnp.tanh(tanh_scale * (v + cubic_term * v * v * v))
    return 0.5 * (1.0 + bent) + 0.5 * v * (1.0 - bent * bent) * tanh_scale * (
        1.0 + 3.0 * cubic_term * v * v
    )


class Sems:
    def __init__(self):
        self.count = 0

    def take(self, n):
        first = self.count
        self.count += n
        return first


SEMS = Sems()
LOAD = SEMS.take(16)
MX_S, MX_R = SEMS.take(1), SEMS.take(1)
MA_S, MA_R = SEMS.take(1), SEMS.take(15)
CX_S, CX_R = SEMS.take(4 * NCH), SEMS.take(4 * NCH)
RS_S, RS_R = SEMS.take(2 * NCH), SEMS.take(30 * NCH)
AG_S, AG_R = SEMS.take(2 * NCH), SEMS.take(30 * NCH)
FW_S, FW_R = SEMS.take(2 * NCH), SEMS.take(32 * NCH)
SX_S, SX_R = SEMS.take(14), SEMS.take(14)
M0_S, M0_R = SEMS.take(1), SEMS.take(31)
XW_S, XW_R = SEMS.take(1), SEMS.take(7)
XF_S, XF_R = SEMS.take(1), SEMS.take(7)
SC_S, SC_R = SEMS.take(1), SEMS.take(7)
OX_S, OX_R = SEMS.take(7), SEMS.take(56)
OF_S, OF_R = SEMS.take(1), SEMS.take(7)


class Cut(Exception):
    pass


def kernel(*refs):
    sends = []
    arrivals = []
    try:
        steps(sends, arrivals, *refs)
    except Cut:
        for wait in arrivals:
            wait()
    for wait in sends:
        wait()


def steps(
    sends, arrivals,
    lat, noi, gt, st, wmod, wup, bup, wdn, bdn, o1, o2,
    latv, noiv, wmodv, wupv, wdnv, bupv, bdnv,
    m0row, m0all, mblk, mpart, mcomb, mall, modv, modx,
    xn, xw, xm, hid, prev, slope_t,
    psend, precv, csum, rsrecv, nbuf, gbuf,
    x_all, sc_all, g_t, h_all, p_all, o_all, pg, hid_t, res,
    sem,
):
    s = lax.axis_index("section")
    t = lax.axis_index("tensor")
    x, yh = s // 2, s % 2
    z, yl, c = t // 4, (t // 2) % 2, t % 2
    q = yl * 2 + c

    def cut(k):
        if STOP == k:
            raise Cut

    def flush():
        for wait in sends:
            wait()
        sends.clear()

    def chip_at(dz, dy):
        return lax.rem(z + dz, 8), lax.rem(yl + dy, 2)

    def chip_dev(dz, dy):
        z2, y2 = chip_at(dz, dy)
        return (s, z2 * 4 + y2 * 2 + c)

    def core_dev(dz, dy, dc):
        z2, y2 = chip_at(dz, dy)
        return (s, z2 * 4 + y2 * 2 + lax.rem(c + dc, 2))

    def sect_at(dx, dy):
        return lax.rem(x + dx, 4) * 2 + lax.rem(yh + dy, 2)

    partner = (s, z * 4 + yl * 2 + (1 - c))

    def remote(src, dst, ssem, rsem, dev):
        return pltpu.make_async_remote_copy(
            src_ref=src, dst_ref=dst, send_sem=sem.at[ssem], recv_sem=sem.at[rsem],
            device_id=dev, device_id_type=MESH,
        )

    def sent(ref, k):
        sends.append(lambda: pltpu.make_async_copy(ref, ref, sem.at[k]).wait())

    if STOP < 0:
        pl.semaphore_signal(pltpu.get_barrier_semaphore(), inc=1, device_id=partner, device_id_type=MESH)
        pl.semaphore_wait(pltpu.get_barrier_semaphore(), 1)
    cut(-1)

    def load(k, src, dst):
        copy = pltpu.make_async_copy(src, dst, sem.at[LOAD + k])
        copy.start()
        arrivals.append(copy.wait)

        def wait():
            arrivals.remove(copy.wait)
            copy.wait()

        return wait

    ld_wmod = load(0, wmod, wmodv)
    ld_lat = load(1, lat, latv.at[:, 0:D])
    ld_up = [load(2, wup.at[0], wupv.at[0])]
    ld_bup = load(3, bup, bupv)
    ld_dn = [load(4, wdn.at[0], wdnv.at[0])]
    ld_bdn = load(5, bdn, bdnv.at[:, 0:D])
    ld_noi = load(6, noi, noiv.at[:, 0:D])
    for n in (1, 2):
        ld_up.append(load(5 + 2 * n, wup.at[n], wupv.at[n]))
        ld_dn.append(load(6 + 2 * n, wdn.at[n], wdnv.at[n]))

    cut(-2)
    barrier = pltpu.get_barrier_semaphore()
    for dz, dy, dc in CORES:
        pl.semaphore_signal(barrier, inc=1, device_id=core_dev(dz, dy, dc), device_id_type=MESH)
    for dx, dy in SECTS:
        pl.semaphore_signal(barrier, inc=1, device_id=(sect_at(dx, dy), t), device_id_type=MESH)

    lane = lax.broadcasted_iota(jnp.int32, (8, 128), 1).astype(f32)
    freq = jnp.exp(lane * (-math.log(10000.0) / 128))

    def embed(stamp):
        angle = stamp.astype(f32) * freq
        return jnp.concatenate([jnp.cos(angle), jnp.sin(angle)], axis=1).astype(bf16)

    emb_gen = embed(gt[s])
    emb_score = embed(st[s])
    sigma = st[s].astype(f32) / TRAIN_STEPS
    ld_wmod()
    row = lax.broadcasted_iota(jnp.int32, (8, MODC), 0)
    m0 = dot(emb_gen, wmodv[0], NT)
    m1 = dot(emb_score, wmodv[1], NT)
    m2 = dot(emb_score, wmodv[2], NT)
    m0row[...] = jnp.zeros_like(m0row)
    m0row[:, 0:MODC] = m0[0:1]
    mblk[...] = jnp.zeros_like(mblk)
    mblk[:, 0:MODC] = jnp.where(row % 4 == 1, m1, jnp.where(row % 4 == 2, m2, 0.0))
    modv[...] = jnp.zeros_like(modv)
    modx[...] = jnp.zeros_like(modx)
    latv[:, D:DP] = jnp.zeros((TOK, DP - D), bf16)
    noiv[:, D:DP] = jnp.zeros((TOK, DP - D), bf16)
    bdnv[:, D:DP] = jnp.zeros((3, DP - D), f32)
    ld_lat()

    def norm_rows(values):
        mean = jnp.mean(values, axis=1, keepdims=True)
        centred = values - mean
        var = jnp.mean(centred * centred, axis=1, keepdims=True)
        return centred * lax.rsqrt(var + 1e-06)

    def norm_body(i, _):
        rows = pl.ds(mul(i, 16), 16)
        normed = norm_rows(latv[rows, 0:D].astype(f32))
        xn[rows, :] = normed
        xw[rows, 0:D] = normed.astype(bf16)
        return 0

    lax.fori_loop(0, 8, norm_body, 0)
    xw[:, D:DP] = jnp.zeros((TOK, DP - D), bf16)
    pl.semaphore_wait(barrier, 38)
    cut(0)

    me = z * 4 + yl * 2 + c
    m0 = []
    for k, (dz, dy, dc) in enumerate(CORES):
        copy = remote(m0row, m0all.at[me], M0_S, M0_R + k, core_dev(dz, dy, dc))
        copy.start()
        m0.append(copy)
    sent(m0all.at[0:31], M0_S)
    mx = remote(mblk, mpart, MX_S, MX_R, partner)
    mx.start()
    sends.append(mx.wait_send)
    m0all[me] = m0row[...]

    def first_lane(section, half):
        return mul((19 * section) // 8 + 2 * half, 128)

    def window_copy(k):
        dev = (sect_at(*SECTS[k]), t)
        return remote(
            xw.at[:, pl.ds(first_lane(dev[0], c), 256)], x_all.at[s, :, pl.ds(mul(c, 256), 256)],
            XW_S, XW_R + k, dev,
        )

    def from_sect(k):
        dx, dy = SECTS[k]
        return sect_at((4 - dx) % 4, dy)

    def window_forward(k):
        part = x_all.at[from_sect(k), :, pl.ds(mul(c, 256), 256)]
        return remote(part, part, XF_S, XF_R + k, partner)

    def scale_copy(k):
        dev = (sect_at(*SECTS[k]), t)
        return remote(modx.at[:, pl.ds(first_lane(dev[0], 0), 512)], sc_all.at[s], SC_S, SC_R + k, dev)

    mx.wait_recv()
    row8 = lax.broadcasted_iota(jnp.int32, (8, 256), 0)
    mcomb[...] = jnp.where((row8 < 4) == (c == 0), mblk[...], mpart[...])
    chip = z * 2 + yl
    ma = []
    for k, (dz, dy) in enumerate(CHIPS):
        copy = remote(mcomb, mall.at[chip], MA_S, MA_R + k, chip_dev(dz, dy))
        copy.start()
        ma.append(copy)
        arrivals.append(copy.wait_recv)
    sent(mall.at[0:15], MA_S)
    mall[chip] = mcomb[...]
    for k in range(7 * BG):
        window_copy(k).start()
        arrivals.append(lambda k=k: window_copy(k).wait_recv())
    if BG:
        sent(x_all.at[0:7, :, 0:256], XW_S)
    x_all[s] = xw[:, pl.ds(first_lane(s, 0), 512)]
    for copy in m0:
        copy.wait_recv()
    for k in range(32):
        modv[0:1, MODC * k : MODC * (k + 1)] = m0all[k, :, 0:MODC]
    cut(1)

    def gen_body(i, _):
        rows = pl.ds(mul(i, 16), 16)
        xm[0, rows, :] = (xn[rows, :] * (1.0 + modv[0:1, D : 2 * D]) + modv[0:1, 0:D]).astype(bf16)
        return 0

    lax.fori_loop(0, 8, gen_body, 0)
    modx[0:1, 0:D] = modv[0:1, D : 2 * D]
    modx[1:2, 0:D] = modv[0:1, 0:D]
    for k in range(7 * BG):
        scale_copy(k).start()
        arrivals.append(lambda k=k: scale_copy(k).wait_recv())
    if BG:
        sent(sc_all.at[0:7], SC_S)
    sc_all[s] = modx[:, pl.ds(first_lane(s, 0), 512)]
    ld_up[0]()
    ld_bup()
    pre = dot(xm[0], wupv[0], NT) + bupv[0:1, :]
    prev[:, 0:F] = pre
    hid[0] = gelu(pre).astype(bf16)
    ld_dn[0]()
    cut(2)

    def chunk_cols(j):
        return BASES[j], min(BASES[j] + 4 * WIDTHS[j], D)

    def all_reduce(a, produce, finish, out, between, on_rows):
        def core_copy(j, i):
            col = mul(BASES[j] // 128 + (i * 2 + 1 - c) * (WIDTHS[j] // 128), 128)
            k = (a * NCH + j) * 2 + i
            return remote(
                psend.at[a, :, pl.ds(col, WIDTHS[j])], precv[a][j].at[i], CX_S + k, CX_R + k, partner
            )

        def scatter(j, k):
            z2, y2 = chip_at(*CHIPS[k])
            i = a * NCH + j
            return remote(
                csum[a][j].at[y2, pl.ds(mul(z2, 16), 16), :], rsrecv[a][j].at[k],
                RS_S + i, RS_R + i * 15 + k, chip_dev(*CHIPS[k]),
            )

        def piece(ref, j, z2, y2):
            col = mul(BASES[j] // 128 + (y2 * 2 + c) * (WIDTHS[j] // 128), 128)
            return ref.at[pl.ds(mul(z2, 16), 16), pl.ds(col, WIDTHS[j])]

        def gather(j, k):
            own = piece(out, j, z, yl)
            i = a * NCH + j
            return remote(own, own, AG_S + i, AG_R + i * 15 + k, chip_dev(*CHIPS[k]))

        def forward(j, k):
            dz, dy = CHIPS[k] if k < 15 else (0, 0)
            z2, y2 = chip_at((8 - dz) % 8, dy)
            part = piece(out, j, z2, y2)
            i = a * NCH + j
            return remote(part, part, FW_S + i, FW_R + i * 16 + k, partner)

        def send_chunk(j):
            for i in range(2):
                core_copy(j, i).wait_recv()
            for i in range(2):
                col = mul(BASES[j] // 128 + (i * 2 + c) * (WIDTHS[j] // 128), 128)
                csum[a][j][i] = (
                    psend[a, :, pl.ds(col, WIDTHS[j])].astype(f32) + precv[a][j][i].astype(f32)
                ).astype(bf16)
            for k in range(15):
                scatter(j, k).start()
            sent(rsrecv[a][j], RS_S + a * NCH + j)

        for j in range(NCH):
            produce(j)
            for i in range(2):
                core_copy(j, i).start()
                sends.append(core_copy(j, i).wait_send)
            if j >= 1:
                send_chunk(j - 1)
        send_chunk(NCH - 1)
        between()
        for j in range(NCH):
            total = csum[a][j][yl, pl.ds(mul(z, 16), 16), :].astype(f32)
            for k in reversed(range(15)):
                scatter(j, k).wait_recv()
                total = total + rsrecv[a][j][k].astype(f32)
            col = mul(BASES[j] // 128 + q * (WIDTHS[j] // 128), 128)
            piece(out, j, z, yl)[...] = finish(total, pl.ds(mul(z, 16), 16), col, WIDTHS[j])
            if STOP == 3 + 3 * a:
                continue
            for k in range(15):
                gather(j, k).start()
            sent(rsrecv[a][j], AG_S + a * NCH + j)
            forward(j, 15).start()
        cut(3 + 3 * a)

        def moves(dz):
            return [CHIPS.index((dz, dy)) if (dz, dy) != (0, 0) else 15 for dy in (0, 1)]

        def finish_rows(dz):
            for j in range(NCH):
                for k in moves(dz):
                    forward(j, k).wait_recv()
            on_rows(lax.rem(z + 8 - dz, 8), dz)

        for step, dz in enumerate(DISTANCES):
            for j in range(NCH):
                for k in moves(dz):
                    if k < 15:
                        gather(j, k).wait_recv()
                        forward(j, k).start()
            if step >= 1:
                finish_rows(DISTANCES[step - 1])
        finish_rows(DISTANCES[-1])
        for j in range(NCH):
            sent(precv[a][j], FW_S + a * NCH + j)

    def produce_gen(j):
        lo, hi = chunk_cols(j)
        psend[0, :, lo:hi] = dot(hid[0], wdnv[0, :, lo:hi], NN).astype(bf16)
        if hi < BASES[j] + 4 * WIDTHS[j]:
            psend[0, :, hi:DP] = jnp.zeros((TOK, DP - hi), bf16)

    def finish_gen(total, rows, col, width):
        cols = pl.ds(col, width)
        gate = modv[0:1, pl.ds(pl.multiple_of(2 * D + col, 128), width)]
        generated = latv[rows, cols].astype(f32) + gate * (total + bdnv[0:1, cols])
        return (
            (1.0 - sigma) * generated + sigma * noiv[rows, cols].astype(f32)
        ).astype(bf16)

    def sect_copy(part, k):
        dev = (sect_at(*SECTS[k]), t)
        i = part * 7 + k
        src = (hid_t, pg)[part]
        dst = (h_all, p_all)[part].at[:, pl.ds(mul(s, 128), 128)]
        return remote(src, dst, SX_S + i, SX_R + i, dev)

    def relay_copy(k):
        dx, dy = SECTS[k]
        part = h_all.at[:, pl.ds(mul(sect_at(0, 1), 128), 128)]
        return remote(part, part, SX_S + k, SX_R + k, (sect_at(dx, 0), t))

    direct = [k for k in range(7) if SECTS[k][1] == 0] + [SECTS.index((0, 1))]
    relayed = [k for k in range(7) if k not in direct]

    def early_sends():
        ld_bdn()
        ld_noi()
        prev[:, F:384] = jnp.zeros((TOK, 384 - F), f32)
        for b in range(3):
            height = min(128, F - 128 * b)
            block = prev[:, 128 * b : 128 * b + 128].T
            slope_t[128 * b : 128 * b + height, :] = slope(block)[0:height]
            hid_t[128 * b : 128 * b + height, :] = gelu(block)[0:height].astype(bf16)
        for k in direct if BG else []:
            sect_copy(0, k).start()
            sends.append(sect_copy(0, k).wait_send)
        h_all[:, pl.ds(mul(s, 128), 128)] = hid_t[...]
        for copy in ma:
            arrivals.remove(copy.wait_recv)
            copy.wait_recv()
        for k in range(32):
            modv[1:3, MODC * k : MODC * (k + 1)] = mall[k // 2, 4 * (k % 2) + 1 : 4 * (k % 2) + 3, 0:MODC]
        for k in reversed(range(7 * BG)):
            window_copy(k).wait_recv()
            window_forward(k).start()
        if BG:
            sent(x_all.at[0:7, :, 0:256], XF_S)

    def relay_hidden():
        if BG:
            sect_copy(0, SECTS.index((0, 1))).wait_recv()
            for k in relayed:
                relay_copy(k).start()
                sends.append(relay_copy(k).wait_send)

    def gather_inputs():
        flush()
        for k in range(7 * BG):
            window_forward(k).wait_recv()
            scale_copy(k).wait_recv()

        def body(i, _):
            values = x_all[i].astype(f32) * (1.0 + sc_all[i, 0:1, :]) + sc_all[i, 1:2, :]
            values = values.astype(bf16).astype(f32)
            for b in range(4):
                block = values[:, 128 * b : 128 * b + 128].T
                g_t[128 * b : 128 * b + 128, pl.ds(mul(i, 128), 128)] = block.astype(bf16)
            return 0

        lax.fori_loop(0, 8, body, 0)

    def score_rows(z2, dz):
        rows = pl.ds(mul(z2, 16), 16)
        normed = norm_rows(nbuf[rows, 0:D].astype(f32))
        for n in (1, 2):
            xm[n, rows, :] = (normed * (1.0 + modv[n : n + 1, D : 2 * D]) + modv[n : n + 1, 0:D]).astype(bf16)

    all_reduce(0, produce_gen, finish_gen, nbuf, early_sends, score_rows)
    relay_hidden()
    cut(4)

    for n in (1, 2):
        ld_up[n]()
        hid[n] = gelu(dot(xm[n], wupv[n], NT) + bupv[n : n + 1, :]).astype(bf16)
    for n in (1, 2):
        ld_dn[n]()
    cut(5)

    def produce_gap(j):
        lo, hi = chunk_cols(j)
        real = dot(hid[1], wdnv[1, :, lo:hi], NN) * modv[1:2, 2 * D + lo : 2 * D + hi]
        fake = dot(hid[2], wdnv[2, :, lo:hi], NN) * modv[2:3, 2 * D + lo : 2 * D + hi]
        psend[1, :, lo:hi] = (fake - real).astype(bf16)
        if hi < BASES[j] + 4 * WIDTHS[j]:
            psend[1, :, hi:DP] = jnp.zeros((TOK, DP - hi), bf16)

    def finish_gap(total, rows, col, width):
        cols = pl.ds(col, width)
        gates = modv[0:3, pl.ds(pl.multiple_of(2 * D + col, 128), width)]
        bias = gates[2:3] * bdnv[2:3, cols] - gates[1:2] * bdnv[1:2, cols]
        return ((total + bias) / 32.0 * gates[0:1]).astype(bf16)

    def slice_copy(z2, dz, k):
        dev = (sect_at(*SECTS[k]), t)
        rows = pl.ds(mul(z2, 16), 16)
        return remote(
            gbuf.at[rows, pl.ds(first_lane(dev[0], c), 256)],
            o_all.at[s, rows, pl.ds(mul(c, 256), 256)],
            OX_S + k, OX_R + 8 * k + dz, dev,
        )

    def slice_forward(k):
        part = o_all.at[from_sect(k), :, pl.ds(mul(c, 256), 256)]
        return remote(part, part, OF_S, OF_R + k, partner)

    def grad_rows(z2, dz):
        for k in range(7 * BG * (1 - LATE)):
            slice_copy(z2, dz, k).start()
            arrivals.append(lambda dz=dz, k=k: slice_copy(z, dz, k).wait_recv())
        rows = pl.ds(mul(z2, 16), 16)
        o_all[s, rows, :] = gbuf[rows, pl.ds(first_lane(s, 0), 512)]

    all_reduce(1, produce_gap, finish_gap, gbuf, gather_inputs, grad_rows)
    for k in range(7 * BG):
        sent(o_all.at[0, :, 0:256], OX_S + k)
    cut(7)

    pg[...] = (dot(wdnv[0], gbuf[:, 0:D], NT) * slope_t[...]).astype(bf16)
    for k in range(7):
        sect_copy(1, k).start()
    if LATE:
        for dz in DISTANCES:
            for k in range(7 * BG):
                slice_copy(lax.rem(z + 8 - dz, 8), dz, k).start()
    p_all[:, pl.ds(mul(s, 128), 128)] = pg[...]
    for k in reversed(range(7 * BG)):
        for dz in DISTANCES:
            slice_copy(z, dz, k).wait_recv()
        slice_forward(k).start()
    flush()
    for k in range(7):
        sends.append(sect_copy(1, k).wait_send)
    if BG:
        sent(o_all.at[0:7, :, 0:256], OF_S)
    for k in reversed(range(7 * BG)):
        (relay_copy(k) if k in relayed else sect_copy(0, k)).wait_recv() if k != SECTS.index((0, 1)) else None
        slice_forward(k).wait_recv()
    wide = dot(h_all[...], o_all[...].reshape(1024, 512), NN)
    shift = lax.rem(48 * s, 128)
    res[1] = pltpu.roll(wide, lax.rem(512 - shift, 512), 1)[:, 0:F].astype(GRAD)
    out2 = pltpu.make_async_copy(res.at[1], o2, sem.at[LOAD + 13])
    out2.start()
    for k in reversed(range(7)):
        sect_copy(1, k).wait_recv()
    res[0] = dot(g_t[pl.ds(pl.multiple_of(shift, 16), F), :], p_all[...], NT).astype(GRAD)
    out1 = pltpu.make_async_copy(res.at[0], o1, sem.at[LOAD + 12])
    out1.start()
    flush()
    out1.wait()
    out2.wait()


def shards(latent_noise, score_noise, gen_time, score_time, w_mod, w_up, b_up, w_down, b_down):
    anywhere = pl.BlockSpec(memory_space=pl.ANY)
    scalars = pl.BlockSpec(memory_space=pltpu.SMEM)
    vm = pltpu.VMEM
    per_chunk = lambda lead: [[vm((lead, TOK, w), bf16) for w in WIDTHS] for _ in range(2)]
    scratch = [
        vm((TOK, DP), bf16), vm((TOK, DP), bf16), vm((3, MODC, 256), bf16),
        vm((3, F, D), bf16), vm((3, F, D), bf16), vm((3, F), f32), vm((3, DP), f32),
        vm((1, 256), f32), vm((32, 1, 256), f32),
        vm((8, 256), f32), vm((8, 256), f32), vm((8, 256), f32), vm((16, 8, 256), f32),
        vm((8, 7424), f32), vm((8, DP), f32),
        vm((TOK, D), f32), vm((TOK, DP), bf16), vm((3, TOK, D), bf16), vm((3, TOK, F), bf16), vm((TOK, 384), f32),
        vm((F, TOK), f32),
        vm((2, TOK, DP), bf16), per_chunk(2), per_chunk(2),
        [[vm((15, 16, w), bf16) for w in WIDTHS] for _ in range(2)],
        vm((TOK, DP), bf16), vm((TOK, DP), bf16),
        vm((8, TOK, 512), bf16), vm((8, 8, 512), f32), vm((512, 1024), bf16),
        vm((F, 1024), bf16), vm((F, 1024), bf16), vm((8, TOK, 512), bf16),
        vm((F, TOK), bf16), vm((F, TOK), bf16), vm((2, F, F), GRAD),
        pltpu.SemaphoreType.DMA((SEMS.count,)),
    ]
    out = jax.ShapeDtypeStruct((F, F), GRAD)
    grads = pl.pallas_call(
        kernel,
        out_shape=(out, out),
        in_specs=[anywhere, anywhere, scalars, scalars] + [anywhere] * 5,
        out_specs=(anywhere, anywhere),
        scratch_shapes=scratch,
        cost_estimate=pl.CostEstimate(flops=1_700_000_000, bytes_accessed=11_000_000, transcendentals=300_000),
        compiler_params=pltpu.CompilerParams(
            collective_id=0, has_side_effects=True, vmem_limit_bytes=56 * 2**20
        ),
    )(
        latent_noise.reshape(TOK, D), score_noise.reshape(TOK, D), gen_time, score_time,
        w_mod.transpose(0, 2, 1), w_up.transpose(0, 2, 1), b_up, w_down, b_down,
    )
    if COPY_OUT:
        return tuple(grad.astype(f32) for grad in grads)
    return grads


def solution(mesh):
    placed = (
        P(None, "section", None),
        P(None, "section", None),
        P(),
        P(),
        P(None, None, "tensor"),
        P(None, None, "tensor"),
        P(None, "tensor"),
        P(None, "tensor", None),
        P(),
    )
    return jax.shard_map(
        shards,
        mesh=mesh,
        in_specs=placed,
        out_specs=(P("section", "tensor"), P("tensor", "section")),
        check_vma=False,
    )
```

time: 96.9 us -> 88.9 us (0.917)
  Pallas kernels: 92.4 us -> 84.5 us
    pallas_call x1, Pallas kernels: 92.4 us -> 84.5 us  [shards(): pl.pallas_call(kernel, out_shape=(out, out), in_specs=[anywhere, anywhere...]
where the time goes in v2:
time: 88.9 us; the launch traced here: 88.7 us
  Pallas kernels  84.5 us (95%)
  local copies, waits for them, and re-layouts  3.64 us (4%)
    pallas_call x1, Pallas kernels, shards(): pl.pallas_call(kernel, out_shape=(out, out), in_specs=[anywhere, anywhere...  84.5 us
    unnamed x2, local copies, waits for them, and re-layouts  3.64 us

profile of v2, /device:TPU:1, one launch (start us, length us, event | category | flops | bytes accessed | tf_op | source)
XLA Modules:
  0.0 88.7 jit_solution(8475725793027754274)
XLA Ops:
  0.6 84.5 %shard_map.104 = (f32[304,304]{1,0:T(8,128)}, f32[304,304]{1,0:T(8,128)}) custom-call(bf16[128,2432]{1,0:T(8,128)(2,1)} %bitcast.5, bf16[128,2432]{1,0:T(8,128)(2,1)} %bitcast.6, s32[8]{0:T(128)} %refs_2_.1, s32[8]{0:T(128)} %refs_3_.1, bf16[3,228,256]{2,1,0:T(8,128)(2,1)} %bitcast.7, bf16[3,304,2432]{2,1,0:T(8,128)(2,1)} %bitcast.4, f32[3,304]{1,0:T(4,128)} %refs_6_.1, ...), custom_call_target="tpu_custom_call" | custom-call | flops 1700000000 | bytes 11000000 | tf_op jit(solution)/shard_map/pallas_call | solution.py:593
  85.1 1.8 %copy.13 = f32[304,304]{1,0:T(8,128)} copy(f32[304,304]{1,0:T(8,128)} %get-tuple-element.4) | data formatting | bytes 739328
  86.9 1.8 %copy.14 = f32[304,304]{1,0:T(8,128)} copy(f32[304,304]{1,0:T(8,128)} %get-tuple-element.5) | data formatting | bytes 739328

commit v3 on v2

--- a/solution.py
+++ b/solution.py
@@ -24,18 +24,13 @@
 DP = 2560
 F = 304
 MODC = 228
-WIDTHS = (384, 256)
-BASES = tuple(4 * sum(WIDTHS[:j]) for j in range(len(WIDTHS)))
-NCH = len(WIDTHS)
+W = DP // 4
 STOP = 99
-COPY_OUT = 0
 BG = 1
-LATE = 0
-GRAD = bf16 if COPY_OUT else f32
-
-DISTANCES = (0, 1, 7, 2, 6, 3, 5, 4)
-CORES = [(dz, dy, dc) for dz in reversed(DISTANCES) for dy in (1, 0) for dc in (0, 1) if (dz, dy, dc) != (0, 0, 0)]
-CHIPS = [(dz, dy) for dz in reversed(DISTANCES) for dy in (1, 0) if (dz, dy) != (0, 0)]
+
+FAR = (4, 3, 5, 2, 6, 1, 7, 0)
+CORES = [(dz, dy, dc) for dz in FAR for dy in (1, 0) for dc in (0, 1) if (dz, dy, dc) != (0, 0, 0)]
+CHIPS = [(dz, dy) for dz in FAR for dy in (1, 0) if (dz, dy) != (0, 0)]
 SECTS = [(2, 1), (1, 1), (3, 1), (2, 0), (0, 1), (1, 0), (3, 0)]
 
 
@@ -72,17 +67,20 @@
 LOAD = SEMS.take(16)
 MX_S, MX_R = SEMS.take(1), SEMS.take(1)
 MA_S, MA_R = SEMS.take(1), SEMS.take(15)
-CX_S, CX_R = SEMS.take(4 * NCH), SEMS.take(4 * NCH)
-RS_S, RS_R = SEMS.take(2 * NCH), SEMS.take(30 * NCH)
-AG_S, AG_R = SEMS.take(2 * NCH), SEMS.take(30 * NCH)
-FW_S, FW_R = SEMS.take(2 * NCH), SEMS.take(32 * NCH)
-SX_S, SX_R = SEMS.take(14), SEMS.take(14)
+CX_S, CX_R = SEMS.take(8), SEMS.take(8)
+RS_S, RS_R = SEMS.take(2), SEMS.take(32)
+AG_S, AG_R = SEMS.take(2), SEMS.take(32)
+FW_S, FW_R = SEMS.take(2), SEMS.take(32)
+SX_S, SX_R = SEMS.take(21), SEMS.take(21)
 M0_S, M0_R = SEMS.take(1), SEMS.take(31)
 XW_S, XW_R = SEMS.take(1), SEMS.take(7)
 XF_S, XF_R = SEMS.take(1), SEMS.take(7)
 SC_S, SC_R = SEMS.take(1), SEMS.take(7)
 OX_S, OX_R = SEMS.take(7), SEMS.take(56)
 OF_S, OF_R = SEMS.take(1), SEMS.take(7)
+
+
+HALVES = ((0, 160), (160, F))
 
 
 class Cut(Exception):
@@ -103,7 +101,7 @@
 
 def steps(
     sends, arrivals,
-    lat, noi, gt, st, wmod, wup, bup, wdn, bdn, o1, o2,
+    lat, noi, gt, st, wmod, wup, bup, wdn, bdn, out,
     latv, noiv, wmodv, wupv, wdnv, bupv, bdnv,
     m0row, m0all, mblk, mpart, mcomb, mall, modv, modx,
     xn, xw, xm, hid, prev, slope_t,
@@ -156,6 +154,22 @@
         pl.semaphore_wait(pltpu.get_barrier_semaphore(), 1)
     cut(-1)
 
+    def row_of(z2):
+        return mul((z2 % 2) * 4 + z2 // 2, 16)
+
+    def load_tokens(k, src, dst):
+        for b in range(8):
+            row = 16 * ((b % 2) * 4 + b // 2)
+            pltpu.make_async_copy(src.at[16 * b : 16 * b + 16, :], dst.at[row : row + 16, 0:D], sem.at[LOAD + k]).start()
+        whole = pltpu.make_async_copy(dst.at[:, 0:D], dst.at[:, 0:D], sem.at[LOAD + k])
+        arrivals.append(whole.wait)
+
+        def wait():
+            arrivals.remove(whole.wait)
+            whole.wait()
+
+        return wait
+
     def load(k, src, dst):
         copy = pltpu.make_async_copy(src, dst, sem.at[LOAD + k])
         copy.start()
@@ -168,12 +182,12 @@
         return wait
 
     ld_wmod = load(0, wmod, wmodv)
-    ld_lat = load(1, lat, latv.at[:, 0:D])
+    ld_lat = load_tokens(1, lat, latv)
     ld_up = [load(2, wup.at[0], wupv.at[0])]
     ld_bup = load(3, bup, bupv)
     ld_dn = [load(4, wdn.at[0], wdnv.at[0])]
     ld_bdn = load(5, bdn, bdnv.at[:, 0:D])
-    ld_noi = load(6, noi, noiv.at[:, 0:D])
+    ld_noi = load_tokens(6, noi, noiv)
     for n in (1, 2):
         ld_up.append(load(5 + 2 * n, wup.at[n], wupv.at[n]))
         ld_dn.append(load(6 + 2 * n, wdn.at[n], wdnv.at[n]))
@@ -209,6 +223,8 @@
     latv[:, D:DP] = jnp.zeros((TOK, DP - D), bf16)
     noiv[:, D:DP] = jnp.zeros((TOK, DP - D), bf16)
     bdnv[:, D:DP] = jnp.zeros((3, DP - D), f32)
+    for a in range(2):
+        psend[a, :, D:DP] = jnp.zeros((TOK, DP - D), bf16)
     ld_lat()
 
     def norm_rows(values):
@@ -309,103 +325,101 @@
     ld_dn[0]()
     cut(2)
 
-    def chunk_cols(j):
-        return BASES[j], min(BASES[j] + 4 * WIDTHS[j], D)
-
-    def all_reduce(a, produce, finish, out, between, on_rows):
-        def core_copy(j, i):
-            col = mul(BASES[j] // 128 + (i * 2 + 1 - c) * (WIDTHS[j] // 128), 128)
-            k = (a * NCH + j) * 2 + i
-            return remote(
-                psend.at[a, :, pl.ds(col, WIDTHS[j])], precv[a][j].at[i], CX_S + k, CX_R + k, partner
-            )
-
-        def scatter(j, k):
-            z2, y2 = chip_at(*CHIPS[k])
-            i = a * NCH + j
-            return remote(
-                csum[a][j].at[y2, pl.ds(mul(z2, 16), 16), :], rsrecv[a][j].at[k],
-                RS_S + i, RS_R + i * 15 + k, chip_dev(*CHIPS[k]),
-            )
-
-        def piece(ref, j, z2, y2):
-            col = mul(BASES[j] // 128 + (y2 * 2 + c) * (WIDTHS[j] // 128), 128)
-            return ref.at[pl.ds(mul(z2, 16), 16), pl.ds(col, WIDTHS[j])]
-
-        def gather(j, k):
-            own = piece(out, j, z, yl)
-            i = a * NCH + j
-            return remote(own, own, AG_S + i, AG_R + i * 15 + k, chip_dev(*CHIPS[k]))
-
-        def forward(j, k):
-            dz, dy = CHIPS[k] if k < 15 else (0, 0)
-            z2, y2 = chip_at((8 - dz) % 8, dy)
-            part = piece(out, j, z2, y2)
-            i = a * NCH + j
-            return remote(part, part, FW_S + i, FW_R + i * 16 + k, partner)
-
-        def send_chunk(j):
-            for i in range(2):
-                core_copy(j, i).wait_recv()
-            for i in range(2):
-                col = mul(BASES[j] // 128 + (i * 2 + c) * (WIDTHS[j] // 128), 128)
-                csum[a][j][i] = (
-                    psend[a, :, pl.ds(col, WIDTHS[j])].astype(f32) + precv[a][j][i].astype(f32)
-                ).astype(bf16)
-            for k in range(15):
-                scatter(j, k).start()
-            sent(rsrecv[a][j], RS_S + a * NCH + j)
-
-        for j in range(NCH):
-            produce(j)
-            for i in range(2):
-                core_copy(j, i).start()
-                sends.append(core_copy(j, i).wait_send)
-            if j >= 1:
-                send_chunk(j - 1)
-        send_chunk(NCH - 1)
-        between()
-        for j in range(NCH):
-            total = csum[a][j][yl, pl.ds(mul(z, 16), 16), :].astype(f32)
-            for k in reversed(range(15)):
-                scatter(j, k).wait_recv()
-                total = total + rsrecv[a][j][k].astype(f32)
-            col = mul(BASES[j] // 128 + q * (WIDTHS[j] // 128), 128)
-            piece(out, j, z, yl)[...] = finish(total, pl.ds(mul(z, 16), 16), col, WIDTHS[j])
-            if STOP == 3 + 3 * a:
-                continue
-            for k in range(15):
-                gather(j, k).start()
-            sent(rsrecv[a][j], AG_S + a * NCH + j)
-            forward(j, 15).start()
-        cut(3 + 3 * a)
-
-        def moves(dz):
-            return [CHIPS.index((dz, dy)) if (dz, dy) != (0, 0) else 15 for dy in (0, 1)]
-
-        def finish_rows(dz):
-            for j in range(NCH):
-                for k in moves(dz):
-                    forward(j, k).wait_recv()
+    def quarter(y2, core):
+        return pl.ds(mul((y2 * 2 + core) * (W // 128), 128), W)
+
+    def core_copy(a, h, i):
+        rows = pl.ds(64 * h, 64)
+        k = (a * 2 + h) * 2 + i
+        return remote(
+            psend.at[a, rows, quarter(i, 1 - c)], precv.at[a, i, rows, :], CX_S + k, CX_R + k, partner
+        )
+
+    def core_send(a, h):
+        for i in range(2):
+            core_copy(a, h, i).start()
+            sends.append(core_copy(a, h, i).wait_send)
+
+    def start_scatter(a, h):
+        rows = pl.ds(64 * h, 64)
+        for i in range(2):
+            core_copy(a, h, i).wait_recv()
+        for i in range(2):
+            csum[a, i, rows, :] = (
+                psend[a, rows, quarter(i, c)].astype(f32) + precv[a, i, rows, :].astype(f32)
+            ).astype(bf16)
+        odd = lax.rem(z + h, 2)
+        for m in (2, 1, 3, 0):
+            for dy in (1, 0):
+                dz = 2 * m + odd
+                z2, y2 = chip_at(dz, dy)
+                copy = remote(
+                    csum.at[a, y2, pl.ds(row_of(z2), 16), :], rsrecv.at[a, dz * 2 + dy],
+                    RS_S + a, RS_R + a * 16 + dz * 2 + dy, chip_dev(dz, dy),
+                )
+                if (m, dy) == (0, 0):
+                    pl.when(odd == 1)(copy.start)
+                else:
+                    copy.start()
+
+    def piece(out, z2, y2):
+        return out.at[pl.ds(row_of(z2), 16), quarter(y2, c)]
+
+    def forward(a, out, dz, dy):
+        z2, y2 = chip_at(8 - dz, dy)
+        part = piece(out, z2, y2)
+        return remote(part, part, FW_S + a, FW_R + a * 16 + dz * 2 + dy, partner)
+
+    def gather(a, out, dz, dy):
+        own = piece(out, z, yl)
+        return remote(own, own, AG_S + a, AG_R + a * 16 + dz * 2 + dy, chip_dev(dz, dy))
+
+    def reduce(a, finish, out):
+        rows = pl.ds(row_of(z), 16)
+        total = csum[a, yl, rows, :].astype(f32)
+        for dz, dy in reversed(CHIPS):
+            slot = rsrecv.at[a, dz * 2 + dy]
+            remote(slot, slot, RS_S + a, RS_R + a * 16 + dz * 2 + dy, partner).wait_recv()
+            total = total + slot[...].astype(f32)
+        sent(rsrecv.at[a, 0:15], RS_S + a)
+        piece(out, z, yl)[...] = finish(total, rows, mul(q * (W // 128), 128), W)
+        for dz, dy in CHIPS:
+            gather(a, out, dz, dy).start()
+        forward(a, out, 0, 0).start()
+        sent(rsrecv.at[a, 0:15], AG_S + a)
+
+    def gather_rows(a, h, out, on_rows):
+        odd = lax.rem(z + h, 2)
+
+        def complete(m):
+            dz = 2 * m + odd
+            for dy in (0, 1):
+                forward(a, out, dz, dy).wait_recv()
             on_rows(lax.rem(z + 8 - dz, 8), dz)
 
-        for step, dz in enumerate(DISTANCES):
-            for j in range(NCH):
-                for k in moves(dz):
-                    if k < 15:
-                        gather(j, k).wait_recv()
-                        forward(j, k).start()
-            if step >= 1:
-                finish_rows(DISTANCES[step - 1])
-        finish_rows(DISTANCES[-1])
-        for j in range(NCH):
-            sent(precv[a][j], FW_S + a * NCH + j)
-
-    def produce_gen(j):
-        lo, hi = chunk_cols(j)
-        psend[0, :, lo:hi] = dot(hid[0], wdnv[0, :, lo:hi], NN).astype(bf16)
-        if hi < BASES[j] + 4 * WIDTHS[j]:
-            psend[0, :, hi:DP] = jnp.zeros((TOK, DP - hi), bf16)
+        before = None
+        for m in (0, 3, 1, 2):
+            dz = 2 * m + odd
+            for dy in (0, 1):
+
+                def pass_on():
+                    gather(a, out, dz, dy).wait_recv()
+                    forward(a, out, dz, dy).start()
+
+                if (m, dy) == (0, 0):
+                    pl.when(odd == 1)(pass_on)
+                else:
+                    pass_on()
+            if before is not None:
+                complete(before)
+            before = m
+        complete(before)
+        if h == 1:
+            sent(precv.at[a], FW_S + a)
+
+    def produce_gen(h):
+        rows = slice(64 * h, 64 * h + 64)
+        psend[0, rows, 0:D] = dot(hid[0, rows], wdnv[0], NN).astype(bf16)
 
     def finish_gen(total, rows, col, width):
         cols = pl.ds(col, width)
@@ -418,8 +432,12 @@
     def sect_copy(part, k):
         dev = (sect_at(*SECTS[k]), t)
         i = part * 7 + k
-        src = (hid_t, pg)[part]
-        dst = (h_all, p_all)[part].at[:, pl.ds(mul(s, 128), 128)]
+        cols = pl.ds(mul(s, 128), 128)
+        if part == 0:
+            src, dst = hid_t, h_all.at[:, cols]
+        else:
+            lo, hi = HALVES[part - 1]
+            src, dst = pg.at[lo:hi, :], p_all.at[lo:hi, cols]
         return remote(src, dst, SX_S + i, SX_R + i, dev)
 
     def relay_copy(k):
@@ -478,29 +496,43 @@
         lax.fori_loop(0, 8, body, 0)
 
     def score_rows(z2, dz):
-        rows = pl.ds(mul(z2, 16), 16)
+        rows = pl.ds(row_of(z2), 16)
         normed = norm_rows(nbuf[rows, 0:D].astype(f32))
         for n in (1, 2):
             xm[n, rows, :] = (normed * (1.0 + modv[n : n + 1, D : 2 * D]) + modv[n : n + 1, 0:D]).astype(bf16)
 
-    all_reduce(0, produce_gen, finish_gen, nbuf, early_sends, score_rows)
+    for h in range(2):
+        produce_gen(h)
+        core_send(0, h)
+    for h in range(2):
+        start_scatter(0, h)
+    early_sends()
+    reduce(0, finish_gen, nbuf)
     relay_hidden()
-    cut(4)
-
-    for n in (1, 2):
-        ld_up[n]()
-        hid[n] = gelu(dot(xm[n], wupv[n], NT) + bupv[n : n + 1, :]).astype(bf16)
-    for n in (1, 2):
-        ld_dn[n]()
-    cut(5)
-
-    def produce_gap(j):
-        lo, hi = chunk_cols(j)
-        real = dot(hid[1], wdnv[1, :, lo:hi], NN) * modv[1:2, 2 * D + lo : 2 * D + hi]
-        fake = dot(hid[2], wdnv[2, :, lo:hi], NN) * modv[2:3, 2 * D + lo : 2 * D + hi]
-        psend[1, :, lo:hi] = (fake - real).astype(bf16)
-        if hi < BASES[j] + 4 * WIDTHS[j]:
-            psend[1, :, hi:DP] = jnp.zeros((TOK, DP - hi), bf16)
+
+    def score_hidden(h):
+        rows = slice(64 * h, 64 * h + 64)
+        for n in (1, 2):
+            hid[n, rows] = gelu(dot(xm[n, rows], wupv[n], NT) + bupv[n : n + 1, :]).astype(bf16)
+
+    def produce_gap(h):
+        rows = slice(64 * h, 64 * h + 64)
+        real = dot(hid[1, rows], wdnv[1], NN) * modv[1:2, 2 * D : 3 * D]
+        fake = dot(hid[2, rows], wdnv[2], NN) * modv[2:3, 2 * D : 3 * D]
+        psend[1, rows, 0:D] = (fake - real).astype(bf16)
+
+    for wait in ld_up[1:] + ld_dn[1:]:
+        wait()
+    gather_rows(0, 0, nbuf, score_rows)
+    score_hidden(0)
+    produce_gap(0)
+    core_send(1, 0)
+    gather_rows(0, 1, nbuf, score_rows)
+    start_scatter(1, 0)
+    score_hidden(1)
+    produce_gap(1)
+    core_send(1, 1)
+    start_scatter(1, 1)
 
     def finish_gap(total, rows, col, width):
         cols = pl.ds(col, width)
@@ -510,7 +542,7 @@
 
     def slice_copy(z2, dz, k):
         dev = (sect_at(*SECTS[k]), t)
-        rows = pl.ds(mul(z2, 16), 16)
+        rows = pl.ds(row_of(z2), 16)
         return remote(
             gbuf.at[rows, pl.ds(first_lane(dev[0], c), 256)],
             o_all.at[s, rows, pl.ds(mul(c, 256), 256)],
@@ -522,32 +554,33 @@
         return remote(part, part, OF_S, OF_R + k, partner)
 
     def grad_rows(z2, dz):
-        for k in range(7 * BG * (1 - LATE)):
+        for k in range(7 * BG):
             slice_copy(z2, dz, k).start()
             arrivals.append(lambda dz=dz, k=k: slice_copy(z, dz, k).wait_recv())
-        rows = pl.ds(mul(z2, 16), 16)
+        rows = pl.ds(row_of(z2), 16)
         o_all[s, rows, :] = gbuf[rows, pl.ds(first_lane(s, 0), 512)]
 
-    all_reduce(1, produce_gap, finish_gap, gbuf, gather_inputs, grad_rows)
+    gather_inputs()
+    reduce(1, finish_gap, gbuf)
+    for h in range(2):
+        gather_rows(1, h, gbuf, grad_rows)
     for k in range(7 * BG):
         sent(o_all.at[0, :, 0:256], OX_S + k)
     cut(7)
 
-    pg[...] = (dot(wdnv[0], gbuf[:, 0:D], NT) * slope_t[...]).astype(bf16)
-    for k in range(7):
-        sect_copy(1, k).start()
-    if LATE:
-        for dz in DISTANCES:
-            for k in range(7 * BG):
-                slice_copy(lax.rem(z + 8 - dz, 8), dz, k).start()
+    for part, (lo, hi) in enumerate(HALVES):
+        pg[lo:hi, :] = (dot(wdnv[0, lo:hi], gbuf[:, 0:D], NT) * slope_t[lo:hi, :]).astype(bf16)
+        for k in range(7):
+            sect_copy(1 + part, k).start()
     p_all[:, pl.ds(mul(s, 128), 128)] = pg[...]
     for k in reversed(range(7 * BG)):
-        for dz in DISTANCES:
+        for dz in reversed(FAR):
             slice_copy(z, dz, k).wait_recv()
         slice_forward(k).start()
     flush()
     for k in range(7):
-        sends.append(sect_copy(1, k).wait_send)
+        for part in (1, 2):
+            sends.append(sect_copy(part, k).wait_send)
     if BG:
         sent(o_all.at[0:7, :, 0:256], OF_S)
     for k in reversed(range(7 * BG)):
@@ -555,13 +588,14 @@
         slice_forward(k).wait_recv()
     wide = dot(h_all[...], o_all[...].reshape(1024, 512), NN)
     shift = lax.rem(48 * s, 128)
-    res[1] = pltpu.roll(wide, lax.rem(512 - shift, 512), 1)[:, 0:F].astype(GRAD)
-    out2 = pltpu.make_async_copy(res.at[1], o2, sem.at[LOAD + 13])
+    res[1] = pltpu.roll(wide, lax.rem(512 - shift, 512), 1)[:, 0:F].astype(bf16)
+    out2 = pltpu.make_async_copy(res.at[1], out.at[1], sem.at[LOAD + 13])
     out2.start()
     for k in reversed(range(7)):
-        sect_copy(1, k).wait_recv()
-    res[0] = dot(g_t[pl.ds(pl.multiple_of(shift, 16), F), :], p_all[...], NT).astype(GRAD)
-    out1 = pltpu.make_async_copy(res.at[0], o1, sem.at[LOAD + 12])
+        for part in (1, 2):
+            sect_copy(part, k).wait_recv()
+    res[0] = dot(g_t[pl.ds(pl.multiple_of(shift, 16), F), :], p_all[...], NT).astype(bf16)
+    out1 = pltpu.make_async_copy(res.at[0], out.at[0], sem.at[LOAD + 12])
     out1.start()
     flush()
     out1.wait()
@@ -572,7 +606,6 @@
     anywhere = pl.BlockSpec(memory_space=pl.ANY)
     scalars = pl.BlockSpec(memory_space=pltpu.SMEM)
     vm = pltpu.VMEM
-    per_chunk = lambda lead: [[vm((lead, TOK, w), bf16) for w in WIDTHS] for _ in range(2)]
     scratch = [
         vm((TOK, DP), bf16), vm((TOK, DP), bf16), vm((3, MODC, 256), bf16),
         vm((3, F, D), bf16), vm((3, F, D), bf16), vm((3, F), f32), vm((3, DP), f32),
@@ -581,20 +614,20 @@
         vm((8, 7424), f32), vm((8, DP), f32),
         vm((TOK, D), f32), vm((TOK, DP), bf16), vm((3, TOK, D), bf16), vm((3, TOK, F), bf16), vm((TOK, 384), f32),
         vm((F, TOK), f32),
-        vm((2, TOK, DP), bf16), per_chunk(2), per_chunk(2),
-        [[vm((15, 16, w), bf16) for w in WIDTHS] for _ in range(2)],
+        vm((2, TOK, DP), bf16), vm((2, 2, TOK, W), bf16), vm((2, 2, TOK, W), bf16),
+        vm((2, 16, 16, W), bf16),
         vm((TOK, DP), bf16), vm((TOK, DP), bf16),
         vm((8, TOK, 512), bf16), vm((8, 8, 512), f32), vm((512, 1024), bf16),
         vm((F, 1024), bf16), vm((F, 1024), bf16), vm((8, TOK, 512), bf16),
-        vm((F, TOK), bf16), vm((F, TOK), bf16), vm((2, F, F), GRAD),
+        vm((F, TOK), bf16), vm((F, TOK), bf16), vm((2, F, F), bf16),
         pltpu.SemaphoreType.DMA((SEMS.count,)),
     ]
-    out = jax.ShapeDtypeStruct((F, F), GRAD)
+    grads_shape = jax.ShapeDtypeStruct((2, F, F), bf16)
     grads = pl.pallas_call(
         kernel,
-        out_shape=(out, out),
+        out_shape=grads_shape,
         in_specs=[anywhere, anywhere, scalars, scalars] + [anywhere] * 5,
-        out_specs=(anywhere, anywhere),
+        out_specs=anywhere,
         scratch_shapes=scratch,
         cost_estimate=pl.CostEstimate(flops=1_700_000_000, bytes_accessed=11_000_000, transcendentals=300_000),
         compiler_params=pltpu.CompilerParams(
@@ -604,9 +637,7 @@
         latent_noise.reshape(TOK, D), score_noise.reshape(TOK, D), gen_time, score_time,
         w_mod.transpose(0, 2, 1), w_up.transpose(0, 2, 1), b_up, w_down, b_down,
     )
-    if COPY_OUT:
-        return tuple(grad.astype(f32) for grad in grads)
-    return grads
+    return grads[0].astype(f32), grads[1].astype(f32)
 
 
 def solution(mesh):

time: 88.9 us -> 83.7 us (0.942)
  local copies, waits for them, and re-layouts: 3.64 us -> 0 us
  Pallas kernels: 84.5 us -> 80.9 us
  other arithmetic: 0 us -> 2.04 us
    unnamed x2 -> x0, local copies, waits for them, and re-layouts: 3.64 us -> none
    pallas_call x1, Pallas kernels: 84.5 us -> 80.9 us  [shards(): pl.pallas_call(kernel, out_shape=grads_shape, in_specs=[anywhere, anywher...]
    convert_element_type x0 -> x1, other arithmetic: none -> 2.04 us  [shards(): return (grads[0].astype(f32), grads[1].astype(f32))]
where the time goes in v3:
time: 83.7 us; the launch traced here: 83.6 us
  Pallas kernels  80.9 us (97%)
  other arithmetic  2.04 us (2%)
    pallas_call x1, Pallas kernels, shards(): pl.pallas_call(kernel, out_shape=grads_shape, in_specs=[anywhere, anywher...  80.9 us
    convert_element_type x1, other arithmetic, shards(): return (grads[0].astype(f32), grads[1].astype(f32))  2.04 us

profile of v3, /device:TPU:1, one launch (start us, length us, event | category | flops | bytes accessed | tf_op | source)
XLA Modules:
  0.0 83.6 jit_solution(3560558629417638913)
XLA Ops:
  0.6 80.9 %shard_map.104 = bf16[2,304,304]{2,1,0:T(8,128)(2,1)} custom-call(bf16[128,2432]{1,0:T(8,128)(2,1)} %bitcast.11, bf16[128,2432]{1,0:T(8,128)(2,1)} %bitcast.12, s32[8]{0:T(128)} %refs_2_.1, s32[8]{0:T(128)} %refs_3_.1, bf16[3,228,256]{2,1,0:T(8,128)(2,1)} %bitcast.13, bf16[3,304,2432]{2,1,0:T(8,128)(2,1)} %bitcast.10, f32[3,304]{1,0:T(4,128)} %refs_6_.1, ...), custom_call_target="tpu_custom_call" | custom-call | flops 1700000000 | bytes 11000000 | tf_op jit(solution)/shard_map/pallas_call | solution.py:626
  81.6 2.0 %bitcast_convert_fusion = (f32[304,304]{1,0:T(8,128)}, f32[304,304]{1,0:T(8,128)}) fusion(bf16[2,304,304]{2,1,0:T(8,128)(2,1)} %shard_map.104), kind=kLoop, calls=%fused_computation | loop fusion | flops 184832 | bytes 1108992 | tf_op jit(solution)/shard_map/convert_element_type | solution.py:640

commit v4 on v3

--- a/solution.py
+++ b/solution.py
@@ -25,12 +25,11 @@
 F = 304
 MODC = 228
 W = DP // 4
-STOP = 99
-BG = 1
 
 FAR = (4, 3, 5, 2, 6, 1, 7, 0)
 CORES = [(dz, dy, dc) for dz in FAR for dy in (1, 0) for dc in (0, 1) if (dz, dy, dc) != (0, 0, 0)]
 CHIPS = [(dz, dy) for dz in FAR for dy in (1, 0) if (dz, dy) != (0, 0)]
+NEAR = (0, 3, 1, 2)
 SECTS = [(2, 1), (1, 1), (3, 1), (2, 0), (0, 1), (1, 0), (3, 0)]
 
 
@@ -71,42 +70,34 @@
 RS_S, RS_R = SEMS.take(2), SEMS.take(32)
 AG_S, AG_R = SEMS.take(2), SEMS.take(32)
 FW_S, FW_R = SEMS.take(2), SEMS.take(32)
-SX_S, SX_R = SEMS.take(21), SEMS.take(21)
+SX_S, SX_R = SEMS.take(9), SEMS.take(21)
 M0_S, M0_R = SEMS.take(1), SEMS.take(31)
 XW_S, XW_R = SEMS.take(1), SEMS.take(7)
 XF_S, XF_R = SEMS.take(1), SEMS.take(7)
 SC_S, SC_R = SEMS.take(1), SEMS.take(7)
 OX_S, OX_R = SEMS.take(7), SEMS.take(56)
-OF_S, OF_R = SEMS.take(1), SEMS.take(7)
-
-
-HALVES = ((0, 160), (160, F))
-
-
-class Cut(Exception):
-    pass
+OY_S, OY_R = SEMS.take(7), SEMS.take(56)
+OF_S, OF_R = SEMS.take(1), SEMS.take(14)
+
+
+SPLIT = 160
 
 
 def kernel(*refs):
     sends = []
-    arrivals = []
-    try:
-        steps(sends, arrivals, *refs)
-    except Cut:
-        for wait in arrivals:
-            wait()
+    steps(sends, *refs)
     for wait in sends:
         wait()
 
 
 def steps(
-    sends, arrivals,
+    sends,
     lat, noi, gt, st, wmod, wup, bup, wdn, bdn, out,
     latv, noiv, wmodv, wupv, wdnv, bupv, bdnv,
     m0row, m0all, mblk, mpart, mcomb, mall, modv, modx,
     xn, xw, xm, hid, prev, slope_t,
     psend, precv, csum, rsrecv, nbuf, gbuf,
-    x_all, sc_all, g_t, h_all, p_all, o_all, pg, hid_t, res,
+    x_all, sc_all, g_t, h_all, p_all, o_all, pg, hid_t,
     sem,
 ):
     s = lax.axis_index("section")
@@ -115,10 +106,6 @@
     z, yl, c = t // 4, (t // 2) % 2, t % 2
     q = yl * 2 + c
 
-    def cut(k):
-        if STOP == k:
-            raise Cut
-
     def flush():
         for wait in sends:
             wait()
@@ -149,55 +136,38 @@
     def sent(ref, k):
         sends.append(lambda: pltpu.make_async_copy(ref, ref, sem.at[k]).wait())
 
-    if STOP < 0:
-        pl.semaphore_signal(pltpu.get_barrier_semaphore(), inc=1, device_id=partner, device_id_type=MESH)
-        pl.semaphore_wait(pltpu.get_barrier_semaphore(), 1)
-    cut(-1)
-
-    def row_of(z2):
-        return mul((z2 % 2) * 4 + z2 // 2, 16)
-
-    def load_tokens(k, src, dst):
-        for b in range(8):
-            row = 16 * ((b % 2) * 4 + b // 2)
-            pltpu.make_async_copy(src.at[16 * b : 16 * b + 16, :], dst.at[row : row + 16, 0:D], sem.at[LOAD + k]).start()
-        whole = pltpu.make_async_copy(dst.at[:, 0:D], dst.at[:, 0:D], sem.at[LOAD + k])
-        arrivals.append(whole.wait)
-
-        def wait():
-            arrivals.remove(whole.wait)
-            whole.wait()
-
-        return wait
-
-    def load(k, src, dst):
-        copy = pltpu.make_async_copy(src, dst, sem.at[LOAD + k])
-        copy.start()
-        arrivals.append(copy.wait)
-
-        def wait():
-            arrivals.remove(copy.wait)
-            copy.wait()
-
-        return wait
-
-    ld_wmod = load(0, wmod, wmodv)
-    ld_lat = load_tokens(1, lat, latv)
-    ld_up = [load(2, wup.at[0], wupv.at[0])]
-    ld_bup = load(3, bup, bupv)
-    ld_dn = [load(4, wdn.at[0], wdnv.at[0])]
-    ld_bdn = load(5, bdn, bdnv.at[:, 0:D])
-    ld_noi = load_tokens(6, noi, noiv)
-    for n in (1, 2):
-        ld_up.append(load(5 + 2 * n, wup.at[n], wupv.at[n]))
-        ld_dn.append(load(6 + 2 * n, wdn.at[n], wdnv.at[n]))
-
-    cut(-2)
     barrier = pltpu.get_barrier_semaphore()
     for dz, dy, dc in CORES:
         pl.semaphore_signal(barrier, inc=1, device_id=core_dev(dz, dy, dc), device_id_type=MESH)
     for dx, dy in SECTS:
         pl.semaphore_signal(barrier, inc=1, device_id=(sect_at(dx, dy), t), device_id_type=MESH)
+
+    pair = z // 2
+
+    def owner(b, y2, h):
+        return 2 * b + lax.rem(y2 + h, 2)
+
+    def block_rows(h, b):
+        return pl.ds(mul(4 * h + lax.rem(b, 2) * 2 + b // 2, 16), 16)
+
+    def rows_of(z2, y2):
+        return block_rows(lax.rem(z2 + y2, 2), z2 // 2)
+
+    def load(k, src, dst):
+        copy = pltpu.make_async_copy(src, dst, sem.at[LOAD + k])
+        copy.start()
+        return copy.wait
+
+    ld_wmod = load(0, wmod, wmodv)
+    ld_lat = load(1, lat, latv.at[:, 0:D])
+    ld_up = [load(2, wup.at[0], wupv.at[0])]
+    ld_bup = load(3, bup, bupv)
+    ld_dn = [load(4, wdn.at[0], wdnv.at[0])]
+    ld_bdn = load(5, bdn, bdnv.at[:, 0:D])
+    ld_noi = load(6, noi, noiv.at[:, 0:D])
+    for n in (1, 2):
+        ld_up.append(load(5 + 2 * n, wup.at[n], wupv.at[n]))
+        ld_dn.append(load(6 + 2 * n, wdn.at[n], wdnv.at[n]))
 
     lane = lax.broadcasted_iota(jnp.int32, (8, 128), 1).astype(f32)
     freq = jnp.exp(lane * (-math.log(10000.0) / 128))
@@ -243,7 +213,6 @@
     lax.fori_loop(0, 8, norm_body, 0)
     xw[:, D:DP] = jnp.zeros((TOK, DP - D), bf16)
     pl.semaphore_wait(barrier, 38)
-    cut(0)
 
     me = z * 4 + yl * 2 + c
     m0 = []
@@ -288,20 +257,16 @@
         copy = remote(mcomb, mall.at[chip], MA_S, MA_R + k, chip_dev(dz, dy))
         copy.start()
         ma.append(copy)
-        arrivals.append(copy.wait_recv)
     sent(mall.at[0:15], MA_S)
     mall[chip] = mcomb[...]
-    for k in range(7 * BG):
+    for k in range(7):
         window_copy(k).start()
-        arrivals.append(lambda k=k: window_copy(k).wait_recv())
-    if BG:
-        sent(x_all.at[0:7, :, 0:256], XW_S)
+    sent(x_all.at[0:7, :, 0:256], XW_S)
     x_all[s] = xw[:, pl.ds(first_lane(s, 0), 512)]
     for copy in m0:
         copy.wait_recv()
     for k in range(32):
         modv[0:1, MODC * k : MODC * (k + 1)] = m0all[k, :, 0:MODC]
-    cut(1)
 
     def gen_body(i, _):
         rows = pl.ds(mul(i, 16), 16)
@@ -311,11 +276,9 @@
     lax.fori_loop(0, 8, gen_body, 0)
     modx[0:1, 0:D] = modv[0:1, D : 2 * D]
     modx[1:2, 0:D] = modv[0:1, 0:D]
-    for k in range(7 * BG):
+    for k in range(7):
         scale_copy(k).start()
-        arrivals.append(lambda k=k: scale_copy(k).wait_recv())
-    if BG:
-        sent(sc_all.at[0:7], SC_S)
+    sent(sc_all.at[0:7], SC_S)
     sc_all[s] = modx[:, pl.ds(first_lane(s, 0), 512)]
     ld_up[0]()
     ld_bup()
@@ -323,7 +286,6 @@
     prev[:, 0:F] = pre
     hid[0] = gelu(pre).astype(bf16)
     ld_dn[0]()
-    cut(2)
 
     def quarter(y2, core):
         return pl.ds(mul((y2 * 2 + core) * (W // 128), 128), W)
@@ -348,22 +310,22 @@
             csum[a, i, rows, :] = (
                 psend[a, rows, quarter(i, c)].astype(f32) + precv[a, i, rows, :].astype(f32)
             ).astype(bf16)
-        odd = lax.rem(z + h, 2)
         for m in (2, 1, 3, 0):
             for dy in (1, 0):
-                dz = 2 * m + odd
-                z2, y2 = chip_at(dz, dy)
+                y2 = lax.rem(yl + dy, 2)
+                z2 = owner(lax.rem(pair + m, 4), y2, h)
+                dz = lax.rem(z2 + 8 - z, 8)
                 copy = remote(
-                    csum.at[a, y2, pl.ds(row_of(z2), 16), :], rsrecv.at[a, dz * 2 + dy],
+                    csum.at[a, y2, rows_of(z2, y2), :], rsrecv.at[a, dz * 2 + dy],
                     RS_S + a, RS_R + a * 16 + dz * 2 + dy, chip_dev(dz, dy),
                 )
                 if (m, dy) == (0, 0):
-                    pl.when(odd == 1)(copy.start)
+                    pl.when(dz != 0)(copy.start)
                 else:
                     copy.start()
 
     def piece(out, z2, y2):
-        return out.at[pl.ds(row_of(z2), 16), quarter(y2, c)]
+        return out.at[rows_of(z2, y2), quarter(y2, c)]
 
     def forward(a, out, dz, dy):
         z2, y2 = chip_at(8 - dz, dy)
@@ -375,7 +337,7 @@
         return remote(own, own, AG_S + a, AG_R + a * 16 + dz * 2 + dy, chip_dev(dz, dy))
 
     def reduce(a, finish, out):
-        rows = pl.ds(row_of(z), 16)
+        rows = rows_of(z, yl)
         total = csum[a, yl, rows, :].astype(f32)
         for dz, dy in reversed(CHIPS):
             slot = rsrecv.at[a, dz * 2 + dy]
@@ -388,34 +350,40 @@
         forward(a, out, 0, 0).start()
         sent(rsrecv.at[a, 0:15], AG_S + a)
 
-    def gather_rows(a, h, out, on_rows):
-        odd = lax.rem(z + h, 2)
-
-        def complete(m):
-            dz = 2 * m + odd
-            for dy in (0, 1):
-                forward(a, out, dz, dy).wait_recv()
-            on_rows(lax.rem(z + 8 - dz, 8), dz)
-
-        before = None
-        for m in (0, 3, 1, 2):
-            dz = 2 * m + odd
-            for dy in (0, 1):
-
-                def pass_on():
-                    gather(a, out, dz, dy).wait_recv()
-                    forward(a, out, dz, dy).start()
-
-                if (m, dy) == (0, 0):
-                    pl.when(odd == 1)(pass_on)
-                else:
-                    pass_on()
-            if before is not None:
-                complete(before)
-            before = m
-        complete(before)
-        if h == 1:
-            sent(precv.at[a], FW_S + a)
+    def source(h, m, dy):
+        z2 = owner(lax.rem(pair + 4 - m, 4), lax.rem(yl + dy, 2), h)
+        return lax.rem(z + 8 - z2, 8)
+
+    def pass_on(a, h, out, m):
+        for dy in (0, 1):
+            dz = source(h, m, dy)
+
+            def step():
+                gather(a, out, dz, dy).wait_recv()
+                forward(a, out, dz, dy).start()
+
+            if (m, dy) == (0, 0):
+                pl.when(dz != 0)(step)
+            else:
+                step()
+
+    def complete(a, h, out, m, on_rows):
+        for dy in (0, 1):
+            forward(a, out, source(h, m, dy), dy).wait_recv()
+        on_rows(h, m, block_rows(h, lax.rem(pair + 4 - m, 4)))
+
+    def gather_first(a, out, on_rows):
+        for step, m in enumerate(NEAR):
+            pass_on(a, 0, out, m)
+            if step > 0:
+                complete(a, 0, out, NEAR[step - 1], on_rows)
+        complete(a, 0, out, NEAR[-1], on_rows)
+
+    def complete_second(a, out, on_rows):
+        for m in NEAR:
+            complete(a, 1, out, m, lambda h, m, rows: None)
+        for m in NEAR:
+            on_rows(1, m, block_rows(1, lax.rem(pair + 4 - m, 4)))
 
     def produce_gen(h):
         rows = slice(64 * h, 64 * h + 64)
@@ -429,16 +397,9 @@
             (1.0 - sigma) * generated + sigma * noiv[rows, cols].astype(f32)
         ).astype(bf16)
 
-    def sect_copy(part, k):
-        dev = (sect_at(*SECTS[k]), t)
-        i = part * 7 + k
+    def hidden_copy(k):
         cols = pl.ds(mul(s, 128), 128)
-        if part == 0:
-            src, dst = hid_t, h_all.at[:, cols]
-        else:
-            lo, hi = HALVES[part - 1]
-            src, dst = pg.at[lo:hi, :], p_all.at[lo:hi, cols]
-        return remote(src, dst, SX_S + i, SX_R + i, dev)
+        return remote(hid_t, h_all.at[:, cols], SX_S + k, SX_R + k, (sect_at(*SECTS[k]), t))
 
     def relay_copy(k):
         dx, dy = SECTS[k]
@@ -448,65 +409,72 @@
     direct = [k for k in range(7) if SECTS[k][1] == 0] + [SECTS.index((0, 1))]
     relayed = [k for k in range(7) if k not in direct]
 
-    def early_sends():
-        ld_bdn()
-        ld_noi()
+    def turn_hidden():
         prev[:, F:384] = jnp.zeros((TOK, 384 - F), f32)
         for b in range(3):
             height = min(128, F - 128 * b)
             block = prev[:, 128 * b : 128 * b + 128].T
             slope_t[128 * b : 128 * b + height, :] = slope(block)[0:height]
             hid_t[128 * b : 128 * b + height, :] = gelu(block)[0:height].astype(bf16)
-        for k in direct if BG else []:
-            sect_copy(0, k).start()
-            sends.append(sect_copy(0, k).wait_send)
+        for k in direct:
+            hidden_copy(k).start()
+            sends.append(hidden_copy(k).wait_send)
         h_all[:, pl.ds(mul(s, 128), 128)] = hid_t[...]
+
+    def other_modulation():
+        ld_bdn()
+        ld_noi()
         for copy in ma:
-            arrivals.remove(copy.wait_recv)
             copy.wait_recv()
         for k in range(32):
             modv[1:3, MODC * k : MODC * (k + 1)] = mall[k // 2, 4 * (k % 2) + 1 : 4 * (k % 2) + 3, 0:MODC]
-        for k in reversed(range(7 * BG)):
+
+    def pass_windows():
+        for k in reversed(range(7)):
             window_copy(k).wait_recv()
             window_forward(k).start()
-        if BG:
-            sent(x_all.at[0:7, :, 0:256], XF_S)
+        sent(x_all.at[0:7, :, 0:256], XF_S)
 
     def relay_hidden():
-        if BG:
-            sect_copy(0, SECTS.index((0, 1))).wait_recv()
-            for k in relayed:
-                relay_copy(k).start()
-                sends.append(relay_copy(k).wait_send)
+        hidden_copy(SECTS.index((0, 1))).wait_recv()
+        for k in relayed:
+            relay_copy(k).start()
+            sends.append(relay_copy(k).wait_send)
 
     def gather_inputs():
         flush()
-        for k in range(7 * BG):
+        for k in range(7):
             window_forward(k).wait_recv()
             scale_copy(k).wait_recv()
 
         def body(i, _):
             values = x_all[i].astype(f32) * (1.0 + sc_all[i, 0:1, :]) + sc_all[i, 1:2, :]
             values = values.astype(bf16).astype(f32)
+            low = lax.broadcasted_iota(jnp.int32, (128, 128), 1) < 64
             for b in range(4):
                 block = values[:, 128 * b : 128 * b + 128].T
-                g_t[128 * b : 128 * b + 128, pl.ds(mul(i, 128), 128)] = block.astype(bf16)
+                turned = pltpu.roll(block, 64, 1)
+                at = (slice(128 * b, 128 * b + 128), pl.ds(mul(i, 128), 128))
+                for h, r, value in ((0, 0, block), (0, 1, turned), (1, 0, turned), (1, 1, block)):
+                    g_t[h, r, at[0], at[1]] = jnp.where(low == (r == 0), value, 0.0).astype(bf16)
             return 0
 
         lax.fori_loop(0, 8, body, 0)
 
-    def score_rows(z2, dz):
-        rows = pl.ds(row_of(z2), 16)
+    def score_rows(h, m, rows):
         normed = norm_rows(nbuf[rows, 0:D].astype(f32))
         for n in (1, 2):
             xm[n, rows, :] = (normed * (1.0 + modv[n : n + 1, D : 2 * D]) + modv[n : n + 1, 0:D]).astype(bf16)
 
-    for h in range(2):
-        produce_gen(h)
-        core_send(0, h)
-    for h in range(2):
-        start_scatter(0, h)
-    early_sends()
+    produce_gen(0)
+    core_send(0, 0)
+    turn_hidden()
+    start_scatter(0, 0)
+    produce_gen(1)
+    core_send(0, 1)
+    other_modulation()
+    start_scatter(0, 1)
+    pass_windows()
     reduce(0, finish_gen, nbuf)
     relay_hidden()
 
@@ -523,11 +491,14 @@
 
     for wait in ld_up[1:] + ld_dn[1:]:
         wait()
-    gather_rows(0, 0, nbuf, score_rows)
+    gather_first(0, nbuf, score_rows)
     score_hidden(0)
+    for m in NEAR:
+        pass_on(0, 1, nbuf, m)
     produce_gap(0)
     core_send(1, 0)
-    gather_rows(0, 1, nbuf, score_rows)
+    complete_second(0, nbuf, score_rows)
+    sent(precv.at[0], FW_S)
     start_scatter(1, 0)
     score_hidden(1)
     produce_gap(1)
@@ -540,66 +511,103 @@
         bias = gates[2:3] * bdnv[2:3, cols] - gates[1:2] * bdnv[1:2, cols]
         return ((total + bias) / 32.0 * gates[0:1]).astype(bf16)
 
-    def slice_copy(z2, dz, k):
+    def slice_copy(h, m, k, last):
         dev = (sect_at(*SECTS[k]), t)
-        rows = pl.ds(row_of(z2), 16)
+        rows = block_rows(h, lax.rem(pair + 4 - m, 4))
+        lo, hi, base, recv = (384, 512, OY_S, OY_R) if last else (0, 384, OX_S, OX_R)
         return remote(
-            gbuf.at[rows, pl.ds(first_lane(dev[0], c), 256)],
-            o_all.at[s, rows, pl.ds(mul(c, 256), 256)],
-            OX_S + k, OX_R + 8 * k + dz, dev,
+            gbuf.at[rows, pl.ds(pl.multiple_of(first_lane(dev[0], 0) + lo, 128), hi - lo)],
+            o_all.at[s, rows, lo:hi], base + k, recv + 8 * k + 4 * h + m, dev,
         )
 
-    def slice_forward(k):
-        part = o_all.at[from_sect(k), :, pl.ds(mul(c, 256), 256)]
-        return remote(part, part, OF_S, OF_R + k, partner)
-
-    def grad_rows(z2, dz):
-        for k in range(7 * BG):
-            slice_copy(z2, dz, k).start()
-            arrivals.append(lambda dz=dz, k=k: slice_copy(z, dz, k).wait_recv())
-        rows = pl.ds(row_of(z2), 16)
+    def is_wide(section):
+        return (section == 2) | (section == 5)
+
+    def grad_rows(h, m, rows):
         o_all[s, rows, :] = gbuf[rows, pl.ds(first_lane(s, 0), 512)]
+
+        @pl.when(c == m % 2)
+        def _():
+            for k in range(7):
+                slice_copy(h, m, k, False).start()
+                pl.when(is_wide(sect_at(*SECTS[k])))(lambda: slice_copy(h, m, k, True).start())
+
+    def slice_forward(h, k):
+        rows = pl.ds(mul(2 * h + lax.rem(pair + c, 2), 32), 32)
+        part = o_all.at[from_sect(k), rows, :]
+        return remote(part, part, OF_S, OF_R + 7 * h + k, partner)
+
+    def pass_slices(h):
+        for k in reversed(range(7)):
+            for u in (0, 1):
+                slice_copy(h, c + 2 * u, k, False).wait_recv()
+                pl.when(is_wide(s))(lambda: slice_copy(h, c + 2 * u, k, True).wait_recv())
+            slice_forward(h, k).start()
+
+    def grad_copy(h, k):
+        dev = (sect_at(*SECTS[k]), t)
+        return remote(
+            pg.at[h], p_all.at[h, :, pl.ds(mul(s, 128), 128)], SX_S + 7 + h, SX_R + 7 * (1 + h) + k, dev
+        )
+
+    def hidden_grad(h):
+        rows = slice(64 * h, 64 * h + 64)
+        value = dot(wdnv[0], gbuf[rows, 0:D], NT) * slope_t[:, rows]
+        rest = jnp.concatenate([value[SPLIT:], jnp.zeros((2 * SPLIT - F, 64), f32)], axis=0)
+        pg[h] = jnp.concatenate([value[0:SPLIT], rest], axis=1).astype(bf16)
+        for k in range(7):
+            grad_copy(h, k).start()
+        p_all[h, :, pl.ds(mul(s, 128), 128)] = pg[h]
 
     gather_inputs()
     reduce(1, finish_gap, gbuf)
-    for h in range(2):
-        gather_rows(1, h, gbuf, grad_rows)
-    for k in range(7 * BG):
-        sent(o_all.at[0, :, 0:256], OX_S + k)
-    cut(7)
-
-    for part, (lo, hi) in enumerate(HALVES):
-        pg[lo:hi, :] = (dot(wdnv[0, lo:hi], gbuf[:, 0:D], NT) * slope_t[lo:hi, :]).astype(bf16)
-        for k in range(7):
-            sect_copy(1 + part, k).start()
-    p_all[:, pl.ds(mul(s, 128), 128)] = pg[...]
-    for k in reversed(range(7 * BG)):
-        for dz in reversed(FAR):
-            slice_copy(z, dz, k).wait_recv()
-        slice_forward(k).start()
+    gather_first(1, gbuf, grad_rows)
+    for m in NEAR:
+        pass_on(1, 1, gbuf, m)
+    hidden_grad(0)
+    complete_second(1, gbuf, grad_rows)
+    hidden_grad(1)
+    sent(precv.at[1], FW_S + 1)
+    for k in range(7):
+        sent(o_all.at[0, 0:64, 0:384], OX_S + k)
+
+    pass_slices(0)
     flush()
+    sent(p_all.at[0, :, 0:896], SX_S + 7)
+    for k in reversed(range(7)):
+        if k != SECTS.index((0, 1)):
+            (relay_copy(k) if k in relayed else hidden_copy(k)).wait_recv()
+    pass_slices(1)
     for k in range(7):
-        for part in (1, 2):
-            sends.append(sect_copy(part, k).wait_send)
-    if BG:
-        sent(o_all.at[0:7, :, 0:256], OF_S)
-    for k in reversed(range(7 * BG)):
-        (relay_copy(k) if k in relayed else sect_copy(0, k)).wait_recv() if k != SECTS.index((0, 1)) else None
-        slice_forward(k).wait_recv()
-    wide = dot(h_all[...], o_all[...].reshape(1024, 512), NN)
-    shift = lax.rem(48 * s, 128)
-    res[1] = pltpu.roll(wide, lax.rem(512 - shift, 512), 1)[:, 0:F].astype(bf16)
-    out2 = pltpu.make_async_copy(res.at[1], out.at[1], sem.at[LOAD + 13])
-    out2.start()
-    for k in reversed(range(7)):
-        for part in (1, 2):
-            sect_copy(part, k).wait_recv()
-    res[0] = dot(g_t[pl.ds(pl.multiple_of(shift, 16), F), :], p_all[...], NT).astype(bf16)
-    out1 = pltpu.make_async_copy(res.at[0], out.at[0], sem.at[LOAD + 12])
-    out1.start()
+
+        @pl.when(is_wide(sect_at(*SECTS[k])))
+        def _():
+            last = o_all.at[0, 0:64, 384:512]
+            pltpu.make_async_copy(last, last, sem.at[OY_S + k]).wait()
+
     flush()
-    out1.wait()
-    out2.wait()
+    sent(o_all.at[0:7, 0:64, :], OF_S)
+    shift = pl.multiple_of(lax.rem(48 * s, 128), 16)
+    rows = pl.ds(shift, F)
+
+    def first_grad(h):
+        for k in reversed(range(7)):
+            grad_copy(h, k).wait_recv()
+        return [dot(g_t[h, r, rows, :], p_all[h], NT) for r in range(2)]
+
+    def second_grad():
+        for h in range(2):
+            for k in reversed(range(7)):
+                slice_forward(h, k).wait_recv()
+        wide = dot(h_all[...], o_all[...].reshape(1024, 512), NN)
+        out[1] = pltpu.roll(wide, lax.rem(512 - shift, 512), 1)[:, 0:F]
+
+    early = first_grad(0)
+    second_grad()
+    sent(p_all.at[1, :, 0:896], SX_S + 8)
+    late = first_grad(1)
+    out[0] = jnp.concatenate([early[0] + late[0], (early[1] + late[1])[:, 0 : F - SPLIT]], axis=1)
+    flush()
 
 
 def shards(latent_noise, score_noise, gen_time, score_time, w_mod, w_up, b_up, w_down, b_down):
@@ -617,17 +625,16 @@
         vm((2, TOK, DP), bf16), vm((2, 2, TOK, W), bf16), vm((2, 2, TOK, W), bf16),
         vm((2, 16, 16, W), bf16),
         vm((TOK, DP), bf16), vm((TOK, DP), bf16),
-        vm((8, TOK, 512), bf16), vm((8, 8, 512), f32), vm((512, 1024), bf16),
-        vm((F, 1024), bf16), vm((F, 1024), bf16), vm((8, TOK, 512), bf16),
-        vm((F, TOK), bf16), vm((F, TOK), bf16), vm((2, F, F), bf16),
+        vm((8, TOK, 512), bf16), vm((8, 8, 512), f32), vm((2, 2, 512, 1024), bf16),
+        vm((F, 1024), bf16), vm((2, SPLIT, 1024), bf16), vm((8, TOK, 512), bf16),
+        vm((2, SPLIT, TOK), bf16), vm((F, TOK), bf16),
         pltpu.SemaphoreType.DMA((SEMS.count,)),
     ]
-    grads_shape = jax.ShapeDtypeStruct((2, F, F), bf16)
     grads = pl.pallas_call(
         kernel,
-        out_shape=grads_shape,
+        out_shape=vm((2, F, F), f32),
         in_specs=[anywhere, anywhere, scalars, scalars] + [anywhere] * 5,
-        out_specs=anywhere,
+        out_specs=pl.BlockSpec(memory_space=pltpu.VMEM),
         scratch_shapes=scratch,
         cost_estimate=pl.CostEstimate(flops=1_700_000_000, bytes_accessed=11_000_000, transcendentals=300_000),
         compiler_params=pltpu.CompilerParams(
@@ -637,7 +644,7 @@
         latent_noise.reshape(TOK, D), score_noise.reshape(TOK, D), gen_time, score_time,
         w_mod.transpose(0, 2, 1), w_up.transpose(0, 2, 1), b_up, w_down, b_down,
     )
-    return grads[0].astype(f32), grads[1].astype(f32)
+    return grads[0], grads[1]
 
 
 def solution(mesh):

time: 83.7 us -> 81.7 us (0.976); the launches traced: 83.6 us -> 80.5 us
  other arithmetic: 2.04 us -> 0 us
  Pallas kernels: 80.9 us -> 78.9 us
  local copies, waits for them, and re-layouts: 0 us -> 0.99 us
    convert_element_type x1 -> x0, other arithmetic: 2.04 us -> none  [shards(): return (grads[0].astype(f32), grads[1].astype(f32))]
    pallas_call x1, Pallas kernels: 80.9 us -> 78.9 us  [shards(): pl.pallas_call(kernel, out_shape=vm((2, F, F), f32), in_specs=[anywhere,...]
    squeeze x0 -> x1, local copies, waits for them, and re-layouts: none -> 0.99 us  [shards(): return (grads[0], grads[1])]
where the time goes in v4:
time: 81.7 us; the launch traced here: 80.5 us
  Pallas kernels  78.9 us (97%)
  local copies, waits for them, and re-layouts  0.99 us (1%)
    pallas_call x1, Pallas kernels, shards(): pl.pallas_call(kernel, out_shape=vm((2, F, F), f32), in_specs=[anywhere,...  78.9 us

profile of v4, /device:TPU:1, one launch (start us, length us, event | category | flops | bytes accessed | tf_op | source)
XLA Modules:
  0.0 80.5 jit_solution(5677513922768194119)
XLA Ops:
  0.6 78.9 %shard_map.104 = f32[2,304,304]{2,1,0:T(8,128)S(1)} custom-call(bf16[128,2432]{1,0:T(8,128)(2,1)} %bitcast.9, bf16[128,2432]{1,0:T(8,128)(2,1)} %bitcast.10, s32[8]{0:T(128)} %refs_2_.1, s32[8]{0:T(128)} %refs_3_.1, bf16[3,228,256]{2,1,0:T(8,128)(2,1)} %bitcast.11, bf16[3,304,2432]{2,1,0:T(8,128)(2,1)} %bitcast.8, f32[3,304]{1,0:T(4,128)} %refs_6_.1, ...), custom_call_target="tpu_custom_call" | custom-call | flops 1700000000 | bytes 11000000 | tf_op jit(solution)/shard_map/pallas_call | solution.py:633
  79.6 1.0 %slice_bitcast_fusion = (f32[304,304]{1,0:T(8,128)}, f32[304,304]{1,0:T(8,128)}) fusion(f32[2,304,304]{2,1,0:T(8,128)S(1)} %shard_map.104), kind=kLoop, calls=%fused_computation | loop fusion | bytes 1478656 | tf_op jit(solution)/shard_map/squeeze | solution.py:647

commit v5 on v4

--- a/solution.py
+++ b/solution.py
@@ -72,7 +72,8 @@
 FW_S, FW_R = SEMS.take(2), SEMS.take(32)
 SX_S, SX_R = SEMS.take(9), SEMS.take(21)
 M0_S, M0_R = SEMS.take(1), SEMS.take(31)
-XW_S, XW_R = SEMS.take(1), SEMS.take(7)
+XW_S, XW_R = SEMS.take(7), SEMS.take(7)
+XV_S, XV_R = SEMS.take(7), SEMS.take(7)
 XF_S, XF_R = SEMS.take(1), SEMS.take(7)
 SC_S, SC_R = SEMS.take(1), SEMS.take(7)
 OX_S, OX_R = SEMS.take(7), SEMS.take(56)
@@ -97,7 +98,7 @@
     m0row, m0all, mblk, mpart, mcomb, mall, modv, modx,
     xn, xw, xm, hid, prev, slope_t,
     psend, precv, csum, rsrecv, nbuf, gbuf,
-    x_all, sc_all, g_t, h_all, p_all, o_all, pg, hid_t,
+    x_all, sc_all, g_t, h_all, h_t, p_all, o_all, pg, hid_t,
     sem,
 ):
     s = lax.axis_index("section")
@@ -162,12 +163,12 @@
     ld_lat = load(1, lat, latv.at[:, 0:D])
     ld_up = [load(2, wup.at[0], wupv.at[0])]
     ld_bup = load(3, bup, bupv)
-    ld_dn = [load(4, wdn.at[0], wdnv.at[0])]
+    ld_dn = [load(4, wdn.at[0], wdnv.at[0, :, 0:D])]
     ld_bdn = load(5, bdn, bdnv.at[:, 0:D])
     ld_noi = load(6, noi, noiv.at[:, 0:D])
     for n in (1, 2):
         ld_up.append(load(5 + 2 * n, wup.at[n], wupv.at[n]))
-        ld_dn.append(load(6 + 2 * n, wdn.at[n], wdnv.at[n]))
+        ld_dn.append(load(6 + 2 * n, wdn.at[n], wdnv.at[n, :, 0:D]))
 
     lane = lax.broadcasted_iota(jnp.int32, (8, 128), 1).astype(f32)
     freq = jnp.exp(lane * (-math.log(10000.0) / 128))
@@ -193,8 +194,8 @@
     latv[:, D:DP] = jnp.zeros((TOK, DP - D), bf16)
     noiv[:, D:DP] = jnp.zeros((TOK, DP - D), bf16)
     bdnv[:, D:DP] = jnp.zeros((3, DP - D), f32)
-    for a in range(2):
-        psend[a, :, D:DP] = jnp.zeros((TOK, DP - D), bf16)
+    for n in range(3):
+        wdnv[n, :, D:DP] = jnp.zeros((F, DP - D), bf16)
     ld_lat()
 
     def norm_rows(values):
@@ -226,14 +227,20 @@
     sends.append(mx.wait_send)
     m0all[me] = m0row[...]
 
-    def first_lane(section, half):
-        return mul((19 * section) // 8 + 2 * half, 128)
-
-    def window_copy(k):
+    def first_lane(section):
+        return mul((19 * section) // 8, 128)
+
+    def is_wide(section):
+        return (section == 2) | (section == 5)
+
+    mine = pl.ds(mul(c, 64), 64)
+
+    def window_copy(k, last):
         dev = (sect_at(*SECTS[k]), t)
+        lo, hi, base, recv = (384, 512, XV_S, XV_R) if last else (0, 384, XW_S, XW_R)
         return remote(
-            xw.at[:, pl.ds(first_lane(dev[0], c), 256)], x_all.at[s, :, pl.ds(mul(c, 256), 256)],
-            XW_S, XW_R + k, dev,
+            xw.at[mine, pl.ds(pl.multiple_of(first_lane(dev[0]) + lo, 128), hi - lo)],
+            x_all.at[s, mine, lo:hi], base + k, recv + k, dev,
         )
 
     def from_sect(k):
@@ -241,12 +248,12 @@
         return sect_at((4 - dx) % 4, dy)
 
     def window_forward(k):
-        part = x_all.at[from_sect(k), :, pl.ds(mul(c, 256), 256)]
+        part = x_all.at[from_sect(k), mine, :]
         return remote(part, part, XF_S, XF_R + k, partner)
 
     def scale_copy(k):
         dev = (sect_at(*SECTS[k]), t)
-        return remote(modx.at[:, pl.ds(first_lane(dev[0], 0), 512)], sc_all.at[s], SC_S, SC_R + k, dev)
+        return remote(modx.at[:, pl.ds(first_lane(dev[0]), 512)], sc_all.at[s], SC_S, SC_R + k, dev)
 
     mx.wait_recv()
     row8 = lax.broadcasted_iota(jnp.int32, (8, 256), 0)
@@ -260,9 +267,10 @@
     sent(mall.at[0:15], MA_S)
     mall[chip] = mcomb[...]
     for k in range(7):
-        window_copy(k).start()
-    sent(x_all.at[0:7, :, 0:256], XW_S)
-    x_all[s] = xw[:, pl.ds(first_lane(s, 0), 512)]
+        window_copy(k, False).start()
+        pl.when(is_wide(sect_at(*SECTS[k])))(lambda: window_copy(k, True).start())
+        sends.append(window_copy(k, False).wait_send)
+    x_all[s] = xw[:, pl.ds(first_lane(s), 512)]
     for copy in m0:
         copy.wait_recv()
     for k in range(32):
@@ -279,13 +287,16 @@
     for k in range(7):
         scale_copy(k).start()
     sent(sc_all.at[0:7], SC_S)
-    sc_all[s] = modx[:, pl.ds(first_lane(s, 0), 512)]
+    sc_all[s] = modx[:, pl.ds(first_lane(s), 512)]
     ld_up[0]()
     ld_bup()
-    pre = dot(xm[0], wupv[0], NT) + bupv[0:1, :]
-    prev[:, 0:F] = pre
-    hid[0] = gelu(pre).astype(bf16)
     ld_dn[0]()
+
+    def gen_hidden(h):
+        rows = slice(64 * h, 64 * h + 64)
+        pre = dot(xm[0, rows], wupv[0], NT) + bupv[0:1, :]
+        prev[rows, 0:F] = pre
+        hid[0, rows] = gelu(pre).astype(bf16)
 
     def quarter(y2, core):
         return pl.ds(mul((y2 * 2 + core) * (W // 128), 128), W)
@@ -297,10 +308,15 @@
             psend.at[a, rows, quarter(i, 1 - c)], precv.at[a, i, rows, :], CX_S + k, CX_R + k, partner
         )
 
-    def core_send(a, h):
-        for i in range(2):
-            core_copy(a, h, i).start()
-            sends.append(core_copy(a, h, i).wait_send)
+    def produce(a, h, value):
+        rows = slice(64 * h, 64 * h + 64)
+        for core in (1 - c, c):
+            for i in range(2):
+                cols = quarter(i, core)
+                psend[a, rows, cols] = value(rows, cols).astype(bf16)
+                if core is not c:
+                    core_copy(a, h, i).start()
+                    sends.append(core_copy(a, h, i).wait_send)
 
     def start_scatter(a, h):
         rows = pl.ds(64 * h, 64)
@@ -385,9 +401,8 @@
         for m in NEAR:
             on_rows(1, m, block_rows(1, lax.rem(pair + 4 - m, 4)))
 
-    def produce_gen(h):
-        rows = slice(64 * h, 64 * h + 64)
-        psend[0, rows, 0:D] = dot(hid[0, rows], wdnv[0], NN).astype(bf16)
+    def gen_value(rows, cols):
+        return dot(hid[0, rows], wdnv[0, :, cols], NN)
 
     def finish_gen(total, rows, col, width):
         cols = pl.ds(col, width)
@@ -431,9 +446,10 @@
 
     def pass_windows():
         for k in reversed(range(7)):
-            window_copy(k).wait_recv()
+            window_copy(k, False).wait_recv()
+            pl.when(is_wide(s))(lambda: window_copy(k, True).wait_recv())
             window_forward(k).start()
-        sent(x_all.at[0:7, :, 0:256], XF_S)
+        sent(x_all.at[0:7, 0:64, :], XF_S)
 
     def relay_hidden():
         hidden_copy(SECTS.index((0, 1))).wait_recv()
@@ -442,7 +458,6 @@
             sends.append(relay_copy(k).wait_send)
 
     def gather_inputs():
-        flush()
         for k in range(7):
             window_forward(k).wait_recv()
             scale_copy(k).wait_recv()
@@ -460,18 +475,28 @@
             return 0
 
         lax.fori_loop(0, 8, body, 0)
+        for k in range(7):
+            if k != SECTS.index((0, 1)):
+                (relay_copy(k) if k in relayed else hidden_copy(k)).wait_recv()
+        for i in range(4):
+            low = lax.broadcasted_iota(jnp.int32, (F, 128), 1) < 64
+            first = h_all[:, 256 * i : 256 * i + 128].astype(f32)
+            second = h_all[:, 256 * i + 128 : 256 * i + 256].astype(f32)
+            cols = slice(128 * i, 128 * i + 128)
+            h_t[0, :, cols] = jnp.where(low, first, pltpu.roll(second, 64, 1)).astype(bf16)
+            h_t[1, :, cols] = jnp.where(low, pltpu.roll(first, 64, 1), second).astype(bf16)
 
     def score_rows(h, m, rows):
         normed = norm_rows(nbuf[rows, 0:D].astype(f32))
         for n in (1, 2):
             xm[n, rows, :] = (normed * (1.0 + modv[n : n + 1, D : 2 * D]) + modv[n : n + 1, 0:D]).astype(bf16)
 
-    produce_gen(0)
-    core_send(0, 0)
+    gen_hidden(0)
+    produce(0, 0, gen_value)
+    gen_hidden(1)
+    start_scatter(0, 0)
+    produce(0, 1, gen_value)
     turn_hidden()
-    start_scatter(0, 0)
-    produce_gen(1)
-    core_send(0, 1)
     other_modulation()
     start_scatter(0, 1)
     pass_windows()
@@ -483,11 +508,11 @@
         for n in (1, 2):
             hid[n, rows] = gelu(dot(xm[n, rows], wupv[n], NT) + bupv[n : n + 1, :]).astype(bf16)
 
-    def produce_gap(h):
-        rows = slice(64 * h, 64 * h + 64)
-        real = dot(hid[1, rows], wdnv[1], NN) * modv[1:2, 2 * D : 3 * D]
-        fake = dot(hid[2, rows], wdnv[2], NN) * modv[2:3, 2 * D : 3 * D]
-        psend[1, rows, 0:D] = (fake - real).astype(bf16)
+    def gap_value(rows, cols):
+        gates = pl.ds(pl.multiple_of(2 * D + cols.start, 128), W)
+        real = dot(hid[1, rows], wdnv[1, :, cols], NN) * modv[1:2, gates]
+        fake = dot(hid[2, rows], wdnv[2, :, cols], NN) * modv[2:3, gates]
+        return fake - real
 
     for wait in ld_up[1:] + ld_dn[1:]:
         wait()
@@ -495,14 +520,12 @@
     score_hidden(0)
     for m in NEAR:
         pass_on(0, 1, nbuf, m)
-    produce_gap(0)
-    core_send(1, 0)
+    produce(1, 0, gap_value)
     complete_second(0, nbuf, score_rows)
     sent(precv.at[0], FW_S)
     start_scatter(1, 0)
     score_hidden(1)
-    produce_gap(1)
-    core_send(1, 1)
+    produce(1, 1, gap_value)
     start_scatter(1, 1)
 
     def finish_gap(total, rows, col, width):
@@ -516,15 +539,12 @@
         rows = block_rows(h, lax.rem(pair + 4 - m, 4))
         lo, hi, base, recv = (384, 512, OY_S, OY_R) if last else (0, 384, OX_S, OX_R)
         return remote(
-            gbuf.at[rows, pl.ds(pl.multiple_of(first_lane(dev[0], 0) + lo, 128), hi - lo)],
+            gbuf.at[rows, pl.ds(pl.multiple_of(first_lane(dev[0]) + lo, 128), hi - lo)],
             o_all.at[s, rows, lo:hi], base + k, recv + 8 * k + 4 * h + m, dev,
         )
 
-    def is_wide(section):
-        return (section == 2) | (section == 5)
-
     def grad_rows(h, m, rows):
-        o_all[s, rows, :] = gbuf[rows, pl.ds(first_lane(s, 0), 512)]
+        o_all[s, rows, :] = gbuf[rows, pl.ds(first_lane(s), 512)]
 
         @pl.when(c == m % 2)
         def _():
@@ -552,15 +572,16 @@
 
     def hidden_grad(h):
         rows = slice(64 * h, 64 * h + 64)
-        value = dot(wdnv[0], gbuf[rows, 0:D], NT) * slope_t[:, rows]
+        value = dot(wdnv[0, :, 0:D], gbuf[rows, 0:D], NT) * slope_t[:, rows]
         rest = jnp.concatenate([value[SPLIT:], jnp.zeros((2 * SPLIT - F, 64), f32)], axis=0)
         pg[h] = jnp.concatenate([value[0:SPLIT], rest], axis=1).astype(bf16)
         for k in range(7):
             grad_copy(h, k).start()
         p_all[h, :, pl.ds(mul(s, 128), 128)] = pg[h]
 
+    flush()
+    reduce(1, finish_gap, gbuf)
     gather_inputs()
-    reduce(1, finish_gap, gbuf)
     gather_first(1, gbuf, grad_rows)
     for m in NEAR:
         pass_on(1, 1, gbuf, m)
@@ -571,23 +592,31 @@
     for k in range(7):
         sent(o_all.at[0, 0:64, 0:384], OX_S + k)
 
+    shift = pl.multiple_of(lax.rem(48 * s, 128), 16)
+
+    def second_grad(h):
+        for k in reversed(range(7)):
+            slice_forward(h, k).wait_recv()
+        return dot(h_t[h], o_all[:, 64 * h : 64 * h + 64, :].reshape(512, 512), NN)
+
+    def store_second(wide):
+        out[1] = pltpu.roll(wide, lax.rem(512 - shift, 512), 1)[:, 0:F]
+
     pass_slices(0)
     flush()
     sent(p_all.at[0, :, 0:896], SX_S + 7)
-    for k in reversed(range(7)):
-        if k != SECTS.index((0, 1)):
-            (relay_copy(k) if k in relayed else hidden_copy(k)).wait_recv()
+    wide_first = second_grad(0)
     pass_slices(1)
     for k in range(7):
 
         @pl.when(is_wide(sect_at(*SECTS[k])))
         def _():
+            window_copy(k, True).wait_send()
             last = o_all.at[0, 0:64, 384:512]
             pltpu.make_async_copy(last, last, sem.at[OY_S + k]).wait()
 
     flush()
     sent(o_all.at[0:7, 0:64, :], OF_S)
-    shift = pl.multiple_of(lax.rem(48 * s, 128), 16)
     rows = pl.ds(shift, F)
 
     def first_grad(h):
@@ -595,15 +624,8 @@
             grad_copy(h, k).wait_recv()
         return [dot(g_t[h, r, rows, :], p_all[h], NT) for r in range(2)]
 
-    def second_grad():
-        for h in range(2):
-            for k in reversed(range(7)):
-                slice_forward(h, k).wait_recv()
-        wide = dot(h_all[...], o_all[...].reshape(1024, 512), NN)
-        out[1] = pltpu.roll(wide, lax.rem(512 - shift, 512), 1)[:, 0:F]
-
     early = first_grad(0)
-    second_grad()
+    store_second(wide_first + second_grad(1))
     sent(p_all.at[1, :, 0:896], SX_S + 8)
     late = first_grad(1)
     out[0] = jnp.concatenate([early[0] + late[0], (early[1] + late[1])[:, 0 : F - SPLIT]], axis=1)
@@ -616,7 +638,7 @@
     vm = pltpu.VMEM
     scratch = [
         vm((TOK, DP), bf16), vm((TOK, DP), bf16), vm((3, MODC, 256), bf16),
-        vm((3, F, D), bf16), vm((3, F, D), bf16), vm((3, F), f32), vm((3, DP), f32),
+        vm((3, F, D), bf16), vm((3, F, DP), bf16), vm((3, F), f32), vm((3, DP), f32),
         vm((1, 256), f32), vm((32, 1, 256), f32),
         vm((8, 256), f32), vm((8, 256), f32), vm((8, 256), f32), vm((16, 8, 256), f32),
         vm((8, 7424), f32), vm((8, DP), f32),
@@ -626,7 +648,7 @@
         vm((2, 16, 16, W), bf16),
         vm((TOK, DP), bf16), vm((TOK, DP), bf16),
         vm((8, TOK, 512), bf16), vm((8, 8, 512), f32), vm((2, 2, 512, 1024), bf16),
-        vm((F, 1024), bf16), vm((2, SPLIT, 1024), bf16), vm((8, TOK, 512), bf16),
+        vm((F, 1024), bf16), vm((2, F, 512), bf16), vm((2, SPLIT, 1024), bf16), vm((8, TOK, 512), bf16),
         vm((2, SPLIT, TOK), bf16), vm((F, TOK), bf16),
         pltpu.SemaphoreType.DMA((SEMS.count,)),
     ]

time: 81.7 us -> 79.5 us (0.973); the launches traced: 80.5 us -> 79.3 us
  Pallas kernels: 78.9 us -> 77.7 us
    pallas_call x1, Pallas kernels: 78.9 us -> 77.7 us  [shards(): pl.pallas_call(kernel, out_shape=vm((2, F, F), f32), in_specs=[anywhere,...]
where the time goes in v5:
time: 79.5 us; the launch traced here: 79.3 us
  Pallas kernels  77.7 us (98%)
  local copies, waits for them, and re-layouts  0.99 us (1%)
    pallas_call x1, Pallas kernels, shards(): pl.pallas_call(kernel, out_shape=vm((2, F, F), f32), in_specs=[anywhere,...  77.7 us

profile of v5, /device:TPU:1, one launch (start us, length us, event | category | flops | bytes accessed | tf_op | source)
XLA Modules:
  0.0 79.3 jit_solution(2223859097968980246)
XLA Ops:
  0.6 77.7 %shard_map.104 = f32[2,304,304]{2,1,0:T(8,128)S(1)} custom-call(bf16[128,2432]{1,0:T(8,128)(2,1)} %bitcast.9, bf16[128,2432]{1,0:T(8,128)(2,1)} %bitcast.10, s32[8]{0:T(128)} %refs_2_.1, s32[8]{0:T(128)} %refs_3_.1, bf16[3,228,256]{2,1,0:T(8,128)(2,1)} %bitcast.11, bf16[3,304,2432]{2,1,0:T(8,128)(2,1)} %bitcast.8, f32[3,304]{1,0:T(4,128)} %refs_6_.1, ...), custom_call_target="tpu_custom_call" | custom-call | flops 1700000000 | bytes 11000000 | tf_op jit(solution)/shard_map/pallas_call | solution.py:655
  78.3 1.0 %slice_bitcast_fusion = (f32[304,304]{1,0:T(8,128)}, f32[304,304]{1,0:T(8,128)}) fusion(f32[2,304,304]{2,1,0:T(8,128)S(1)} %shard_map.104), kind=kLoop, calls=%fused_computation | loop fusion | bytes 1478656 | tf_op jit(solution)/shard_map/squeeze | solution.py:669

commit v6 on v5

--- a/solution.py
+++ b/solution.py
@@ -70,7 +70,7 @@
 RS_S, RS_R = SEMS.take(2), SEMS.take(32)
 AG_S, AG_R = SEMS.take(2), SEMS.take(32)
 FW_S, FW_R = SEMS.take(2), SEMS.take(32)
-SX_S, SX_R = SEMS.take(9), SEMS.take(21)
+SX_S, SX_R = SEMS.take(8), SEMS.take(14)
 M0_S, M0_R = SEMS.take(1), SEMS.take(31)
 XW_S, XW_R = SEMS.take(7), SEMS.take(7)
 XV_S, XV_R = SEMS.take(7), SEMS.take(7)
@@ -79,6 +79,8 @@
 OX_S, OX_R = SEMS.take(7), SEMS.take(56)
 OY_S, OY_R = SEMS.take(7), SEMS.take(56)
 OF_S, OF_R = SEMS.take(1), SEMS.take(14)
+ZX_S, ZX_R = SEMS.take(1), SEMS.take(7)
+PA_S, PA_R = SEMS.take(2), SEMS.take(14)
 
 
 SPLIT = 160
@@ -105,7 +107,7 @@
     t = lax.axis_index("tensor")
     x, yh = s // 2, s % 2
     z, yl, c = t // 4, (t // 2) % 2, t % 2
-    q = yl * 2 + c
+    q = c * 2 + yl
 
     def flush():
         for wait in sends:
@@ -299,7 +301,7 @@
         hid[0, rows] = gelu(pre).astype(bf16)
 
     def quarter(y2, core):
-        return pl.ds(mul((y2 * 2 + core) * (W // 128), 128), W)
+        return pl.ds(mul((core * 2 + y2) * (W // 128), 128), W)
 
     def core_copy(a, h, i):
         rows = pl.ds(64 * h, 64)
@@ -311,12 +313,11 @@
     def produce(a, h, value):
         rows = slice(64 * h, 64 * h + 64)
         for core in (1 - c, c):
-            for i in range(2):
-                cols = quarter(i, core)
-                psend[a, rows, cols] = value(rows, cols).astype(bf16)
-                if core is not c:
-                    core_copy(a, h, i).start()
-                    sends.append(core_copy(a, h, i).wait_send)
+            cols = pl.ds(mul(core * (2 * W // 128), 128), 2 * W)
+            psend[a, rows, cols] = value(rows, cols).astype(bf16)
+            for i in range(2) if core is not c else []:
+                core_copy(a, h, i).start()
+                sends.append(core_copy(a, h, i).wait_send)
 
     def start_scatter(a, h):
         rows = pl.ds(64 * h, 64)
@@ -509,7 +510,7 @@
             hid[n, rows] = gelu(dot(xm[n, rows], wupv[n], NT) + bupv[n : n + 1, :]).astype(bf16)
 
     def gap_value(rows, cols):
-        gates = pl.ds(pl.multiple_of(2 * D + cols.start, 128), W)
+        gates = pl.ds(pl.multiple_of(2 * D + cols.start, 128), 2 * W)
         real = dot(hid[1, rows], wdnv[1, :, cols], NN) * modv[1:2, gates]
         fake = dot(hid[2, rows], wdnv[2, :, cols], NN) * modv[2:3, gates]
         return fake - real
@@ -543,6 +544,14 @@
             o_all.at[s, rows, lo:hi], base + k, recv + 8 * k + 4 * h + m, dev,
         )
 
+    beside_of = lax.rem(z, 2)
+
+    def slice_beside(k):
+        rows = block_rows(0, lax.rem(pair + 4 - c - 2 * beside_of, 4))
+        part = o_all.at[from_sect(k), rows, :]
+        dev = (s, (z + 1 - 2 * beside_of) * 4 + yl * 2 + c)
+        return remote(part, part, ZX_S, ZX_R + k, dev)
+
     def grad_rows(h, m, rows):
         o_all[s, rows, :] = gbuf[rows, pl.ds(first_lane(s), 512)]
 
@@ -557,26 +566,75 @@
         part = o_all.at[from_sect(k), rows, :]
         return remote(part, part, OF_S, OF_R + 7 * h + k, partner)
 
+    def wait_slices(h, k, m):
+        slice_copy(h, m, k, False).wait_recv()
+        pl.when(is_wide(s))(lambda: slice_copy(h, m, k, True).wait_recv())
+
+    def share_slices():
+        for k in reversed(range(7)):
+            wait_slices(0, k, c + 2 * beside_of)
+            slice_beside(k).start()
+        sent(o_all.at[0:7, 0:16, :], ZX_S)
+
     def pass_slices(h):
         for k in reversed(range(7)):
-            for u in (0, 1):
-                slice_copy(h, c + 2 * u, k, False).wait_recv()
-                pl.when(is_wide(s))(lambda: slice_copy(h, c + 2 * u, k, True).wait_recv())
+            wait_slices(h, k, c)
+            wait_slices(h, k, c + 2)
             slice_forward(h, k).start()
 
-    def grad_copy(h, k):
-        dev = (sect_at(*SECTS[k]), t)
+    def grad_copy(k):
+        cols = pl.ds(mul(s, 128), 128)
         return remote(
-            pg.at[h], p_all.at[h, :, pl.ds(mul(s, 128), 128)], SX_S + 7 + h, SX_R + 7 * (1 + h) + k, dev
+            pg.at[1], p_all.at[1, :, cols], SX_S + 7, SX_R + 7 + k, (sect_at(*SECTS[k]), t)
         )
+
+    RELAY = ((0, 64), (64, SPLIT))
+    across = SECTS.index((0, 1))
+
+    def first_copy(part, k):
+        rows = slice(*RELAY[part])
+        cols = pl.ds(mul(s, 128), 128)
+        return remote(
+            pg.at[0, rows], p_all.at[0, rows, cols], PA_S + part, PA_R + 7 * part + k, (sect_at(*SECTS[k]), t)
+        )
+
+    def first_relay(part, k):
+        rows = slice(*RELAY[part])
+        dx = SECTS[k][0]
+        origin = sect_at(0, 1) if part == 0 else sect_at((4 - dx) % 4, 0)
+        dev = sect_at(dx, 0) if part == 0 else sect_at(0, 1)
+        block = p_all.at[0, rows, pl.ds(mul(origin, 128), 128)]
+        return remote(block, block, PA_S + part, PA_R + 7 * part + k, (dev, t))
+
+    def relay_first():
+        first_copy(0, across).wait_recv()
+        for k in relayed:
+            first_relay(0, k).start()
+        for k in relayed:
+            first_copy(1, SECTS.index((SECTS[k][0], 0))).wait_recv()
+            first_relay(1, k).start()
+        for part in range(2):
+            sent(p_all.at[0, RELAY[part][0] : RELAY[part][1], 0:896], PA_S + part)
+
+    def wait_first():
+        for k in direct:
+            if k != across:
+                first_copy(0, k).wait_recv()
+        first_copy(1, across).wait_recv()
+        for part in range(2):
+            for k in relayed:
+                first_relay(part, k).wait_recv()
 
     def hidden_grad(h):
         rows = slice(64 * h, 64 * h + 64)
         value = dot(wdnv[0, :, 0:D], gbuf[rows, 0:D], NT) * slope_t[:, rows]
         rest = jnp.concatenate([value[SPLIT:], jnp.zeros((2 * SPLIT - F, 64), f32)], axis=0)
         pg[h] = jnp.concatenate([value[0:SPLIT], rest], axis=1).astype(bf16)
-        for k in range(7):
-            grad_copy(h, k).start()
+        for k in range(7) if h == 1 else []:
+            grad_copy(k).start()
+        for part in range(2) if h == 0 else []:
+            for k in direct:
+                first_copy(part, k).start()
         p_all[h, :, pl.ds(mul(s, 128), 128)] = pg[h]
 
     flush()
@@ -602,11 +660,10 @@
     def store_second(wide):
         out[1] = pltpu.roll(wide, lax.rem(512 - shift, 512), 1)[:, 0:F]
 
+    relay_first()
     pass_slices(0)
+    pass_slices(1)
     flush()
-    sent(p_all.at[0, :, 0:896], SX_S + 7)
-    wide_first = second_grad(0)
-    pass_slices(1)
     for k in range(7):
 
         @pl.when(is_wide(sect_at(*SECTS[k])))
@@ -620,14 +677,18 @@
     rows = pl.ds(shift, F)
 
     def first_grad(h):
-        for k in reversed(range(7)):
-            grad_copy(h, k).wait_recv()
+        if h == 0:
+            wait_first()
+        else:
+            for k in reversed(range(7)):
+                grad_copy(k).wait_recv()
         return [dot(g_t[h, r, rows, :], p_all[h], NT) for r in range(2)]
 
+    wide_first = second_grad(0)
+    sent(p_all.at[1, :, 0:896], SX_S + 7)
+    late = first_grad(1)
+    store_second(wide_first + second_grad(1))
     early = first_grad(0)
-    store_second(wide_first + second_grad(1))
-    sent(p_all.at[1, :, 0:896], SX_S + 8)
-    late = first_grad(1)
     out[0] = jnp.concatenate([early[0] + late[0], (early[1] + late[1])[:, 0 : F - SPLIT]], axis=1)
     flush()
 

time: 79.5 us -> 78 us (0.981)
  Pallas kernels: 77.7 us -> 76.3 us
    pallas_call x1, Pallas kernels: 77.7 us -> 76.3 us  [shards(): pl.pallas_call(kernel, out_shape=vm((2, F, F), f32), in_specs=[anywhere,...]
where the time goes in v6:
time: 78 us
  Pallas kernels  76.3 us (98%)
  local copies, waits for them, and re-layouts  0.99 us (1%)
    pallas_call x1, Pallas kernels, shards(): pl.pallas_call(kernel, out_shape=vm((2, F, F), f32), in_specs=[anywhere,...  76.3 us

profile of v6, /device:TPU:1, one launch (start us, length us, event | category | flops | bytes accessed | tf_op | source)
XLA Modules:
  0.0 78.0 jit_solution(14916965546206285180)
XLA Ops:
  0.6 76.3 %shard_map.104 = f32[2,304,304]{2,1,0:T(8,128)S(1)} custom-call(bf16[128,2432]{1,0:T(8,128)(2,1)} %bitcast.9, bf16[128,2432]{1,0:T(8,128)(2,1)} %bitcast.10, s32[8]{0:T(128)} %refs_2_.1, s32[8]{0:T(128)} %refs_3_.1, bf16[3,228,256]{2,1,0:T(8,128)(2,1)} %bitcast.11, bf16[3,304,2432]{2,1,0:T(8,128)(2,1)} %bitcast.8, f32[3,304]{1,0:T(4,128)} %refs_6_.1, ...), custom_call_target="tpu_custom_call" | custom-call | flops 1700000000 | bytes 11000000 | tf_op jit(solution)/shard_map/pallas_call | solution.py:716
  77.0 1.0 %slice_bitcast_fusion = (f32[304,304]{1,0:T(8,128)}, f32[304,304]{1,0:T(8,128)}) fusion(f32[2,304,304]{2,1,0:T(8,128)S(1)} %shard_map.104), kind=kLoop, calls=%fused_computation | loop fusion | bytes 1478656 | tf_op jit(solution)/shard_map/squeeze | solution.py:730

commit v7 on v6

--- a/solution.py
+++ b/solution.py
@@ -268,10 +268,14 @@
         ma.append(copy)
     sent(mall.at[0:15], MA_S)
     mall[chip] = mcomb[...]
-    for k in range(7):
-        window_copy(k, False).start()
-        pl.when(is_wide(sect_at(*SECTS[k])))(lambda: window_copy(k, True).start())
-        sends.append(window_copy(k, False).wait_send)
+    def send_windows(dy):
+        for k in range(7):
+            if SECTS[k][1] == dy:
+                window_copy(k, False).start()
+                pl.when(is_wide(sect_at(*SECTS[k])))(lambda: window_copy(k, True).start())
+                sends.append(window_copy(k, False).wait_send)
+
+    send_windows(0)
     x_all[s] = xw[:, pl.ds(first_lane(s), 512)]
     for copy in m0:
         copy.wait_recv()
@@ -500,7 +504,6 @@
     turn_hidden()
     other_modulation()
     start_scatter(0, 1)
-    pass_windows()
     reduce(0, finish_gen, nbuf)
     relay_hidden()
 
@@ -518,6 +521,7 @@
     for wait in ld_up[1:] + ld_dn[1:]:
         wait()
     gather_first(0, nbuf, score_rows)
+    send_windows(1)
     score_hidden(0)
     for m in NEAR:
         pass_on(0, 1, nbuf, m)
@@ -639,6 +643,7 @@
 
     flush()
     reduce(1, finish_gap, gbuf)
+    pass_windows()
     gather_inputs()
     gather_first(1, gbuf, grad_rows)
     for m in NEAR:

time: 78 us -> 77.5 us (level)
  no operation moved by 1% of the time
where the time goes in v7:
time: 77.5 us; the launch traced here: 77.4 us
  Pallas kernels  75.8 us (98%)
  local copies, waits for them, and re-layouts  0.99 us (1%)
    pallas_call x1, Pallas kernels, shards(): pl.pallas_call(kernel, out_shape=vm((2, F, F), f32), in_specs=[anywhere,...  75.8 us

profile of v7, /device:TPU:1, one launch (start us, length us, event | category | flops | bytes accessed | tf_op | source)
XLA Modules:
  0.0 77.4 jit_solution(7336443531044181865)
XLA Ops:
  0.6 75.8 %shard_map.104 = f32[2,304,304]{2,1,0:T(8,128)S(1)} custom-call(bf16[128,2432]{1,0:T(8,128)(2,1)} %bitcast.9, bf16[128,2432]{1,0:T(8,128)(2,1)} %bitcast.10, s32[8]{0:T(128)} %refs_2_.1, s32[8]{0:T(128)} %refs_3_.1, bf16[3,228,256]{2,1,0:T(8,128)(2,1)} %bitcast.11, bf16[3,304,2432]{2,1,0:T(8,128)(2,1)} %bitcast.8, f32[3,304]{1,0:T(4,128)} %refs_6_.1, ...), custom_call_target="tpu_custom_call" | custom-call | flops 1700000000 | bytes 11000000 | tf_op jit(solution)/shard_map/pallas_call | solution.py:721
  76.5 1.0 %slice_bitcast_fusion = (f32[304,304]{1,0:T(8,128)}, f32[304,304]{1,0:T(8,128)}) fusion(f32[2,304,304]{2,1,0:T(8,128)S(1)} %shard_map.104), kind=kLoop, calls=%fused_computation | loop fusion | bytes 1478656 | tf_op jit(solution)/shard_map/squeeze | solution.py:735
